TPU v7x, 32 devices: a whole 2x2x4 slice. The times are simulated.
32 devices in a mesh: shard: 2 (over x), ctx: 4 (over y, core), tp: 4 (over z).
Axes of the slice: x: 2, y: 2, z: 4, core: 2. Of those that a mesh axis runs over, the one named last changes fastest.
Arguments:
- inputs: bfloat16 [2, 2048, 2048], P('shard', 'ctx'), may hold values from -6 to 6
- lengths: int32 [2], P('shard'), may hold values from 1024 to 2048, as said below
- cotangent: bfloat16 [2, 2048, 2048], P('shard', 'ctx'), may hold values from -6 to 6
- norm1_gain: bfloat16 [2048], P(('shard', 'ctx')), may hold values from 0.099609375 to 1.8984375
- branch_weight: bfloat16 [2048, 2560], P(('shard', 'ctx'), 'tp'), may hold values from -0.125 to 0.125
- rec_in_weight: bfloat16 [2048, 2560], P(('shard', 'ctx'), 'tp'), may hold values from -0.125 to 0.125
- conv_weight: bfloat16 [4, 16, 160], P(None, 'tp', ('shard', 'ctx')), may hold values from -3 to 3
- conv_bias: bfloat16 [16, 160], P('tp', ('shard', 'ctx')), may hold values from -3 to 3
- rgate_weight: bfloat16 [16, 160, 160], P('tp', ('shard', 'ctx')), may hold values from -0.5 to 0.5
- rgate_bias: bfloat16 [16, 160], P('tp', ('shard', 'ctx')), may hold values from -3 to 3
- igate_weight: bfloat16 [16, 160, 160], P('tp', ('shard', 'ctx')), may hold values from -0.5 to 0.5
- igate_bias: bfloat16 [16, 160], P('tp', ('shard', 'ctx')), may hold values from -3 to 3
- decay_param: bfloat16 [16, 160], P('tp', ('shard', 'ctx')), may hold values from 4.5 to 8.5
- out_weight: bfloat16 [2048, 2560], P(('shard', 'ctx'), 'tp'), may hold values from -0.5 to 0.5
- norm2_gain: bfloat16 [2048], P(('shard', 'ctx')), may hold values from 0.099609375 to 1.8984375
- mlp_gate_weight: bfloat16 [2048, 6144], P(('shard', 'ctx'), 'tp'), may hold values from -0.125 to 0.125
- mlp_up_weight: bfloat16 [2048, 6144], P(('shard', 'ctx'), 'tp'), may hold values from -0.125 to 0.125
- mlp_down_weight: bfloat16 [2048, 6144], P(('shard', 'ctx'), 'tp'), may hold values from -0.109375 to 0.109375
Outputs:
- output: bfloat16 [2, 2048, 2048], P('shard', 'ctx')
- input_grad: bfloat16 [2, 2048, 2048], P('shard', 'ctx')
- grad_norm1_gain: float32 [2048], P(('shard', 'ctx'))
- grad_branch_weight: float32 [2048, 2560], P(('shard', 'ctx'), 'tp')
- grad_rec_in_weight: float32 [2048, 2560], P(('shard', 'ctx'), 'tp')
- grad_conv_weight: float32 [4, 16, 160], P(None, 'tp', ('shard', 'ctx'))
- grad_conv_bias: float32 [16, 160], P('tp', ('shard', 'ctx'))
- grad_rgate_weight: float32 [16, 160, 160], P('tp', ('shard', 'ctx'))
- grad_rgate_bias: float32 [16, 160], P('tp', ('shard', 'ctx'))
- grad_igate_weight: float32 [16, 160, 160], P('tp', ('shard', 'ctx'))
- grad_igate_bias: float32 [16, 160], P('tp', ('shard', 'ctx'))
- grad_decay_param: float32 [16, 160], P('tp', ('shard', 'ctx'))
- grad_out_weight: float32 [2048, 2560], P(('shard', 'ctx'), 'tp')
- grad_norm2_gain: float32 [2048], P(('shard', 'ctx'))
- grad_mlp_gate_weight: float32 [2048, 6144], P(('shard', 'ctx'), 'tp')
- grad_mlp_up_weight: float32 [2048, 6144], P(('shard', 'ctx'), 'tp')
- grad_mlp_down_weight: float32 [2048, 6144], P(('shard', 'ctx'), 'tp')
Inputs may be any that keep to these rules, and one draw needn't show every extreme that they name: `lengths`: some slot holds exactly 2048 tokens and another exactly 1024.
All inputs are finite; a program needn't handle non-finite values.
Results may differ from a plain program's by a relative error of at most 0.008.
The roundings to bfloat16 on the way count: a program that leaves them out, or rounds other values in their place, can miss the bound.
Values may be sent and summed in bfloat16 or wider, within the bound.
A program may use at most 192 MiB of HBM per device.

v0:
```python
import math

import jax
import jax.numpy as jnp
from jax import lax
from jax.sharding import PartitionSpec as P

EPS = 1e-06
DECAY_SCALE = 8.0
HIGHEST = lax.Precision.HIGHEST


def shifted(value, axis, steps):
    count = lax.axis_size(axis)
    first, last = (max(0, -steps), min(count, count - steps))
    return lax.ppermute(value, axis, [(source, source + steps) for source in range(first, last)])


def entering(x, axis, combine, identity, reverse):
    size, mine = (lax.axis_size(axis), lax.axis_index(axis))
    everything = jax.tree.map(lambda part: lax.all_gather(part, axis), x)
    start = jax.tree.map(
        lambda part, zero: jnp.broadcast_to(jnp.asarray(zero, part.dtype), part.shape), x, identity
    )

    def turn(k, before):
        at = size - 1 - k if reverse else k
        reached = at > mine if reverse else at < mine
        new = combine(before, jax.tree.map(lambda part: part[at], everything))
        return jax.tree.map(lambda a, b: jnp.where(reached, a, b), new, before)

    return lax.fori_loop(0, size, turn, start)


def affine_join(earlier, later):
    return (earlier[0] * later[0], later[0] * earlier[1] + later[1])


def norm_apply(tok_rows, gain_row):
    return (
        tok_rows * lax.rsqrt(jnp.mean(tok_rows * tok_rows, axis=-1, keepdims=True) + EPS) * gain_row
    )


def conv_apply(extended, conv_taps, conv_shift):
    tap_count = conv_taps.shape[0]
    row_count = extended.shape[1] - tap_count + 1
    flat_taps = conv_taps.reshape(tap_count, -1)
    result = conv_shift.reshape(-1) + jnp.zeros_like(extended[:, :row_count])
    for tap_index in range(tap_count):
        start_row = tap_count - 1 - tap_index
        result = result + flat_taps[tap_index] * extended[:, start_row : start_row + row_count]
    return result


def block_dense(blocks):
    group_count, block_width = (blocks.shape[0], blocks.shape[1])
    selector = jnp.eye(group_count, dtype=jnp.float32)
    dense = blocks[:, :, None, :] * selector[:, None, :, None]
    return dense.reshape(group_count * block_width, group_count * block_width)


def gate_apply(conv_out, w_rate, b_rate, w_entry, b_entry, decay_param):
    rate_dense = block_dense(w_rate)
    entry_dense = block_dense(w_entry)
    gate_rate = jax.nn.sigmoid(
        jnp.einsum("stc,cd->std", conv_out, rate_dense, precision=HIGHEST) + b_rate.reshape(-1)
    )
    gate_entry = jax.nn.sigmoid(
        jnp.einsum("stc,cd->std", conv_out, entry_dense, precision=HIGHEST) + b_entry.reshape(-1)
    )
    log_decay = -DECAY_SCALE * gate_rate * jax.nn.softplus(-decay_param.reshape(-1))
    decay_rows = jnp.exp(log_decay)
    drive_rows = jnp.sqrt(-jnp.expm1(2.0 * log_decay)) * gate_entry * conv_out
    return (decay_rows, drive_rows)


def block_scan(decay_rows, drive_rows, reverse):
    slot_count, row_count, channels = decay_rows.shape
    piece = math.gcd(row_count, 16)
    pieces = row_count // piece
    logs = jnp.log(decay_rows).reshape(slot_count, pieces, piece, channels)
    drive = drive_rows.reshape(slot_count, pieces, piece, channels)
    rows_i = jnp.arange(piece, dtype=jnp.int32)[:, None]
    rows_j = jnp.arange(piece, dtype=jnp.int32)[None, :]
    if reverse:
        within = (rows_j >= rows_i).astype(jnp.float32)
        edge = 0
    else:
        within = (rows_j <= rows_i).astype(jnp.float32)
        edge = piece - 1
    cumul = jnp.einsum("tu,snuc->sntc", within, logs, precision=HIGHEST)
    spread = cumul[:, :, :, None, :] - cumul[:, :, None, :, :]
    weights = jnp.where(within[:, :, None] > 0.5, jnp.exp(jnp.minimum(spread, 0.0)), 0.0)
    inner = jnp.sum(weights * drive[:, :, None, :, :], axis=3)
    inner_decay = jnp.exp(cumul)
    part_decay = inner_decay[:, :, edge]
    part_state = inner[:, :, edge]
    total_decay, total_state = lax.associative_scan(
        affine_join, (part_decay, part_state), axis=1, reverse=reverse
    )
    ones_row = jnp.ones_like(total_decay[:, :1])
    zeros_row = jnp.zeros_like(total_state[:, :1])
    if reverse:
        before_decay = jnp.concatenate([total_decay[:, 1:], ones_row], axis=1)
        before_state = jnp.concatenate([total_state[:, 1:], zeros_row], axis=1)
    else:
        before_decay = jnp.concatenate([ones_row, total_decay[:, :-1]], axis=1)
        before_state = jnp.concatenate([zeros_row, total_state[:, :-1]], axis=1)
    run_decay = inner_decay * before_decay[:, :, None]
    run_state = inner + inner_decay * before_state[:, :, None]
    return (
        run_decay.reshape(slot_count, row_count, channels),
        run_state.reshape(slot_count, row_count, channels),
    )


def mix_apply(branch_pre, state_rows):
    return jax.nn.gelu(branch_pre) * state_rows


def dot_rows(left_side, right_side):
    return lax.dot_general(
        left_side, right_side, (((1,), (1,)), ((), ())), preferred_element_type=jnp.float32
    )


def dot_tokens(left_side, right_side):
    return lax.dot_general(
        left_side, right_side, (((0,), (0,)), ((), ())), preferred_element_type=jnp.float32
    )


def local(
    inputs,
    lengths,
    cotangent,
    norm1_gain,
    branch_weight,
    rec_in_weight,
    conv_weight,
    conv_bias,
    rgate_weight,
    rgate_bias,
    igate_weight,
    igate_bias,
    decay_param,
    out_weight,
    norm2_gain,
    mlp_gate_weight,
    mlp_up_weight,
    mlp_down_weight,
):
    slot_count, block_len, model_width = inputs.shape
    gathered = (
        lax.all_gather(norm1_gain, ("shard", "ctx"), axis=0, tiled=True),
        lax.all_gather(branch_weight, ("shard", "ctx"), axis=0, tiled=True),
        lax.all_gather(rec_in_weight, ("shard", "ctx"), axis=0, tiled=True),
        lax.all_gather(conv_weight, ("shard", "ctx"), axis=2, tiled=True),
        lax.all_gather(conv_bias, ("shard", "ctx"), axis=1, tiled=True),
        lax.all_gather(rgate_weight, ("shard", "ctx"), axis=1, tiled=True),
        lax.all_gather(rgate_bias, ("shard", "ctx"), axis=1, tiled=True),
        lax.all_gather(igate_weight, ("shard", "ctx"), axis=1, tiled=True),
        lax.all_gather(igate_bias, ("shard", "ctx"), axis=1, tiled=True),
        lax.all_gather(decay_param, ("shard", "ctx"), axis=1, tiled=True),
        lax.all_gather(out_weight, ("shard", "ctx"), axis=0, tiled=True),
        lax.all_gather(norm2_gain, ("shard", "ctx"), axis=0, tiled=True),
        lax.all_gather(mlp_gate_weight, ("shard", "ctx"), axis=0, tiled=True),
        lax.all_gather(mlp_up_weight, ("shard", "ctx"), axis=0, tiled=True),
        lax.all_gather(mlp_down_weight, ("shard", "ctx"), axis=0, tiled=True),
    )
    (
        gain_one,
        w_branch,
        w_rec,
        conv_taps,
        conv_shift,
        w_rate,
        b_rate,
        w_entry,
        b_entry,
        decay_full,
        w_out,
        gain_two,
        w_gate,
        w_up,
        w_down,
    ) = gathered
    gain_one_f = gain_one.astype(jnp.float32)
    gain_two_f = gain_two.astype(jnp.float32)
    taps_f = conv_taps.astype(jnp.float32)
    shift_f = conv_shift.astype(jnp.float32)
    rate_f = w_rate.astype(jnp.float32)
    rate_bias_f = b_rate.astype(jnp.float32)
    entry_f = w_entry.astype(jnp.float32)
    entry_bias_f = b_entry.astype(jnp.float32)
    decay_f = decay_full.astype(jnp.float32)
    positions = lax.axis_index("ctx") * block_len + jnp.arange(block_len, dtype=jnp.int32)
    live_mask = (positions[None, :] < lengths[:, None]).astype(jnp.float32)
    live_rows = live_mask.reshape(-1, 1)
    tok_rows = inputs.reshape(-1, model_width).astype(jnp.float32)
    low_one = norm_apply(tok_rows, gain_one_f).astype(jnp.bfloat16)
    branch_pre = jnp.dot(low_one, w_branch, preferred_element_type=jnp.float32)
    rec_pre = jnp.dot(low_one, w_rec, preferred_element_type=jnp.float32)
    channels = rec_pre.shape[1]
    rec_blocks = rec_pre.reshape(slot_count, block_len, channels)
    edge_count = conv_taps.shape[0] - 1
    edge_rows = shifted(rec_blocks[:, block_len - edge_count :], "ctx", 1)
    extended = jnp.concatenate([edge_rows, rec_blocks], axis=1)
    conv_out = conv_apply(extended, taps_f, shift_f)
    decay_rows, drive_rows = gate_apply(
        conv_out, rate_f, rate_bias_f, entry_f, entry_bias_f, decay_f
    )
    run_decay, run_state = block_scan(decay_rows, drive_rows, False)
    last_decay = run_decay[:, -1]
    last_state = run_state[:, -1]
    incoming = entering(
        (last_decay, last_state),
        "ctx",
        affine_join,
        (jnp.ones_like(last_decay), jnp.zeros_like(last_state)),
        False,
    )
    start_state = incoming[1]
    state_blocks = run_state + run_decay * start_state[:, None]
    state_rows = state_blocks.reshape(-1, channels)
    mixed_low = mix_apply(branch_pre, state_rows).astype(jnp.bfloat16)
    middle = tok_rows + lax.psum(dot_rows(mixed_low, w_out), "tp")
    low_two = norm_apply(middle, gain_two_f).astype(jnp.bfloat16)
    gate_pre = jnp.dot(low_two, w_gate, preferred_element_type=jnp.float32)
    up_pre = jnp.dot(low_two, w_up, preferred_element_type=jnp.float32)
    hidden_low = (jax.nn.gelu(gate_pre) * up_pre).astype(jnp.bfloat16)
    final_rows = (middle + lax.psum(dot_rows(hidden_low, w_down), "tp")) * live_rows
    output = final_rows.astype(jnp.bfloat16).reshape(slot_count, block_len, model_width)
    regathered = (
        lax.all_gather(norm1_gain, ("shard", "ctx"), axis=0, tiled=True),
        lax.all_gather(branch_weight, ("shard", "ctx"), axis=0, tiled=True),
        lax.all_gather(rec_in_weight, ("shard", "ctx"), axis=0, tiled=True),
        lax.all_gather(conv_weight, ("shard", "ctx"), axis=2, tiled=True),
        lax.all_gather(conv_bias, ("shard", "ctx"), axis=1, tiled=True),
        lax.all_gather(rgate_weight, ("shard", "ctx"), axis=1, tiled=True),
        lax.all_gather(rgate_bias, ("shard", "ctx"), axis=1, tiled=True),
        lax.all_gather(igate_weight, ("shard", "ctx"), axis=1, tiled=True),
        lax.all_gather(igate_bias, ("shard", "ctx"), axis=1, tiled=True),
        lax.all_gather(decay_param, ("shard", "ctx"), axis=1, tiled=True),
        lax.all_gather(out_weight, ("shard", "ctx"), axis=0, tiled=True),
        lax.all_gather(norm2_gain, ("shard", "ctx"), axis=0, tiled=True),
        lax.all_gather(mlp_gate_weight, ("shard", "ctx"), axis=0, tiled=True),
        lax.all_gather(mlp_up_weight, ("shard", "ctx"), axis=0, tiled=True),
        lax.all_gather(mlp_down_weight, ("shard", "ctx"), axis=0, tiled=True),
    )
    (
        gain_one,
        w_branch,
        w_rec,
        conv_taps,
        conv_shift,
        w_rate,
        b_rate,
        w_entry,
        b_entry,
        decay_full,
        w_out,
        gain_two,
        w_gate,
        w_up,
        w_down,
    ) = regathered
    gain_one_f = gain_one.astype(jnp.float32)
    gain_two_f = gain_two.astype(jnp.float32)
    taps_f = conv_taps.astype(jnp.float32)
    shift_f = conv_shift.astype(jnp.float32)
    rate_f = w_rate.astype(jnp.float32)
    rate_bias_f = b_rate.astype(jnp.float32)
    entry_f = w_entry.astype(jnp.float32)
    entry_bias_f = b_entry.astype(jnp.float32)
    decay_f = decay_full.astype(jnp.float32)
    grad_final = cotangent.reshape(-1, model_width).astype(jnp.float32) * live_rows
    grad_low = grad_final.astype(jnp.bfloat16)
    grad_w_down = dot_tokens(grad_low, hidden_low)
    grad_hidden = jnp.dot(grad_low, w_down, preferred_element_type=jnp.float32)
    gate_grad = (
        grad_hidden * up_pre * jax.grad(lambda values: jnp.sum(jax.nn.gelu(values)))(gate_pre)
    )
    gate_low = gate_grad.astype(jnp.bfloat16)
    up_low = (grad_hidden * jax.nn.gelu(gate_pre)).astype(jnp.bfloat16)
    grad_w_gate = dot_tokens(low_two, gate_low)
    grad_w_up = dot_tokens(low_two, up_low)
    two_partial = dot_rows(gate_low, w_gate) + dot_rows(up_low, w_up)
    _, norm_two_pull = jax.vjp(norm_apply, middle, gain_two_f)
    grad_normed_two = lax.psum(two_partial, "tp")
    middle_norm_grad, grad_gain_two = norm_two_pull(grad_normed_two)
    grad_middle = grad_final + middle_norm_grad
    middle_low = grad_middle.astype(jnp.bfloat16)
    grad_w_out = dot_tokens(middle_low, mixed_low)
    grad_mixed = jnp.dot(middle_low, w_out, preferred_element_type=jnp.float32)
    _, mix_pull = jax.vjp(mix_apply, branch_pre, state_rows)
    branch_grad, state_grad = mix_pull(grad_mixed)
    branch_low = branch_grad.astype(jnp.bfloat16)
    state_grad = state_grad.reshape(slot_count, block_len, channels)
    next_decay = jnp.concatenate([decay_rows[:, 1:], jnp.ones_like(decay_rows[:, :1])], axis=1)
    back_decay, back_grad = block_scan(next_decay, state_grad, True)
    first_decay = decay_rows[:, 0]
    outgoing = (first_decay * back_decay[:, 0], first_decay * back_grad[:, 0])
    arriving = entering(
        outgoing,
        "ctx",
        affine_join,
        (jnp.ones_like(outgoing[0]), jnp.zeros_like(outgoing[1])),
        True,
    )
    carried = back_grad + back_decay * arriving[1][:, None]
    previous = jnp.concatenate([start_state[:, None], state_blocks[:, :-1]], axis=1)
    _, gate_pull = jax.vjp(
        gate_apply, conv_out, rate_f, rate_bias_f, entry_f, entry_bias_f, decay_f
    )
    conv_grad, grad_w_rate, grad_b_rate, grad_w_entry, grad_b_entry, grad_decay = gate_pull(
        (carried * previous, carried)
    )
    _, conv_pull = jax.vjp(conv_apply, extended, taps_f, shift_f)
    extended_grad, grad_taps, grad_shift = conv_pull(conv_grad)
    returned = shifted(extended_grad[:, :edge_count], "ctx", -1)
    rec_grad = extended_grad[:, edge_count:] + jnp.concatenate(
        [jnp.zeros((slot_count, block_len - edge_count, channels), jnp.float32), returned], axis=1
    )
    rec_low = rec_grad.reshape(-1, channels).astype(jnp.bfloat16)
    grad_w_branch = dot_tokens(low_one, branch_low)
    grad_w_rec = dot_tokens(low_one, rec_low)
    one_partial = dot_rows(branch_low, w_branch) + dot_rows(rec_low, w_rec)
    grad_normed_one = lax.psum(one_partial, "tp")
    _, norm_one_pull = jax.vjp(norm_apply, tok_rows, gain_one_f)
    rows_norm_grad, grad_gain_one = norm_one_pull(grad_normed_one)
    input_grad = (
        (grad_middle + rows_norm_grad)
        .astype(jnp.bfloat16)
        .reshape(slot_count, block_len, model_width)
    )
    reduced = (
        lax.psum_scatter(grad_gain_one, ("shard", "ctx"), scatter_dimension=0, tiled=True),
        lax.psum_scatter(grad_w_branch, ("shard", "ctx"), scatter_dimension=0, tiled=True),
        lax.psum_scatter(grad_w_rec, ("shard", "ctx"), scatter_dimension=0, tiled=True),
        lax.psum_scatter(grad_taps, ("shard", "ctx"), scatter_dimension=2, tiled=True),
        lax.psum_scatter(grad_shift, ("shard", "ctx"), scatter_dimension=1, tiled=True),
        lax.psum_scatter(grad_w_rate, ("shard", "ctx"), scatter_dimension=1, tiled=True),
        lax.psum_scatter(grad_b_rate, ("shard", "ctx"), scatter_dimension=1, tiled=True),
        lax.psum_scatter(grad_w_entry, ("shard", "ctx"), scatter_dimension=1, tiled=True),
        lax.psum_scatter(grad_b_entry, ("shard", "ctx"), scatter_dimension=1, tiled=True),
        lax.psum_scatter(grad_decay, ("shard", "ctx"), scatter_dimension=1, tiled=True),
        lax.psum_scatter(grad_w_out, ("shard", "ctx"), scatter_dimension=0, tiled=True),
        lax.psum_scatter(grad_gain_two, ("shard", "ctx"), scatter_dimension=0, tiled=True),
        lax.psum_scatter(grad_w_gate, ("shard", "ctx"), scatter_dimension=0, tiled=True),
        lax.psum_scatter(grad_w_up, ("shard", "ctx"), scatter_dimension=0, tiled=True),
        lax.psum_scatter(grad_w_down, ("shard", "ctx"), scatter_dimension=0, tiled=True),
    )
    return (output, input_grad) + tuple(reduced)


def solution(mesh):
    placed = (
        P("shard", "ctx", None),
        P("shard"),
        P("shard", "ctx", None),
        P(("shard", "ctx")),
        P(("shard", "ctx"), "tp"),
        P(("shard", "ctx"), "tp"),
        P(None, "tp", ("shard", "ctx")),
        P("tp", ("shard", "ctx")),
        P("tp", ("shard", "ctx"), None),
        P("tp", ("shard", "ctx")),
        P("tp", ("shard", "ctx"), None),
        P("tp", ("shard", "ctx")),
        P("tp", ("shard", "ctx")),
        P(("shard", "ctx"), "tp"),
        P(("shard", "ctx")),
        P(("shard", "ctx"), "tp"),
        P(("shard", "ctx"), "tp"),
        P(("shard", "ctx"), "tp"),
    )
    return jax.shard_map(
        local,
        mesh=mesh,
        in_specs=placed,
        out_specs=(
            P("shard", "ctx", None),
            P("shard", "ctx", None),
            P(("shard", "ctx")),
            P(("shard", "ctx"), "tp"),
            P(("shard", "ctx"), "tp"),
            P(None, "tp", ("shard", "ctx")),
            P("tp", ("shard", "ctx")),
            P("tp", ("shard", "ctx"), None),
            P("tp", ("shard", "ctx")),
            P("tp", ("shard", "ctx"), None),
            P("tp", ("shard", "ctx")),
            P("tp", ("shard", "ctx")),
            P(("shard", "ctx"), "tp"),
            P(("shard", "ctx")),
            P(("shard", "ctx"), "tp"),
            P(("shard", "ctx"), "tp"),
            P(("shard", "ctx"), "tp"),
        ),
        check_vma=False,
    )
```

profile of v0, /device:TPU:0, one launch (start us, length us, event | category | flops | bytes accessed | tf_op | source)
XLA Modules:
  0.0 1710.8 jit_solution(8709612178492862646)
XLA Ops:
  12.8 10.3 all-gather
  23.3 9.2 all_gather.76
  41.4 9.6 all_gather.81
  51.0 9.6 all_gather.78
  60.6 8.7 all-gather.2
  69.3 8.1 all-gather.3
  78.8 8.7 all-gather.4
  139.1 8.5 multiply_reduce_fusion.1
  193.7 8.3 pad.392
  215.2 8.3 pad.393
  258.3 8.1 all-gather.5
  267.1 143.9 %all-reduce.71.cloned.1.call-done = f32[512,2048]{1,0:T(8,128)} async-done(((f32[512,2048]{1,0:T(8,128)}), f32[512,2048]{1,0:T(8,128)}) %all-reduce.71.cloned.1.call-update) | async-done | bytes 4194320 | tf_op jit(solution)/shard_map/psum | solution.py:228
  417.5 39.9 %all-gather.19.cloned.1.call-done = bf16[2048,1536]{1,0:T(8,128)(2,1)} async-done(((bf16[256,1536]{1,0:T(8,128)(2,1)}), bf16[2048,1536]{1,0:T(8,128)(2,1)}) %all-gather.19.cloned.1.call-update) | async-done | bytes 6291472 | tf_op jit(solution)/shard_map/all_gather | solution.py:168
  457.4 8.5 fusion.137
  465.9 38.9 %all-gather.21.cloned.1.call-done = bf16[2048,1536]{1,0:T(8,128)(2,1)} async-done(((bf16[256,1536]{1,0:T(8,128)(2,1)}), bf16[2048,1536]{1,0:T(8,128)(2,1)}) %all-gather.21.cloned.1.call-update) | async-done | bytes 6291472 | tf_op jit(solution)/shard_map/all_gather | solution.py:169
  504.9 8.6 fusion.138
  513.4 39.0 %all-gather.23.cloned.1.call-done = bf16[2048,1536]{1,0:T(8,128)(2,1)} async-done(((bf16[256,1536]{1,0:T(8,128)(2,1)}), bf16[2048,1536]{1,0:T(8,128)(2,1)}) %all-gather.23.cloned.1.call-update) | async-done | bytes 6291472 | tf_op jit(solution)/shard_map/all_gather | solution.py:170
  552.5 11.8 multiply_convert_fusion.2
  595.4 135.9 %all-reduce.73.cloned.1.call-done = f32[512,2048]{1,0:T(8,128)} async-done(((f32[512,2048]{1,0:T(8,128)}), f32[512,2048]{1,0:T(8,128)}) %all-reduce.73.cloned.1.call-update) | async-done | bytes 4194320 | tf_op jit(solution)/shard_map/psum | solution.py:291
  744.2 8.1 multiply_reduce_fusion
  811.6 8.2 pad.395
  910.0 10.1 fusion.142
  920.3 10.1 fusion.143
  931.1 10.2 fusion.79
  947.5 286.3 %all-reduce.77.cloned.1.call-done = (f32[512,2048]{1,0:T(8,128)}, f32[512,2048]{1,0:T(8,128)}) async-done(((f32[512,2048]{1,0:T(8,128)}, f32[512,2048]{1,0:T(8,128)}), (f32[512,2048]{1,0:T(8,128)}, f32[512,2048]{1,0:T(8,128)})) %all-reduce.77.cloned.1.call-update) | async-done | bytes 8388624 | tf_op jit(solution)/shard_map/psum | solution.py:233
  1237.3 24.5 %all-reduce.63 = (f32[2048]{0:T(1024)S(1)}, f32[4,4,160]{2,1,0:T(4,128)S(1)}, f32[4,160]{1,0:T(4,128)S(1)}, f32[4,160]{1,0:T(4,128)S(1)}, f32[4,160]{1,0:T(4,128...) all-reduce(f32[2048]{0:T(1024)S(1)} %get-tuple-element.283, ...), channel_id=2, replica_groups=mesh['shard'=2,'ctx'=4,'tp'=4] {'shard','ctx'}, use_global_device_ids=true, to_apply=%region_15.16.clone | all-reduce | flops 9216 | bytes 73728
  1275.6 18.1 %reduce-scatter.16.cloned.1.call-done = f32[256,640]{1,0:T(8,128)} async-done(((f32[2048,640]{1,0:T(8,128)}), f32[256,640]{1,0:T(8,128)}) %reduce-scatter.16.cloned.1.call-update) | async-done | bytes 655376 | tf_op jit(solution)/shard_map/reduce_scatter | solution.py:349
  1293.7 60.4 %reduce-scatter.12.cloned.1.call-done = f32[256,640]{1,0:T(8,128)} async-done(((f32[2048,640]{1,0:T(8,128)}), f32[256,640]{1,0:T(8,128)}) %reduce-scatter.12.cloned.1.call-update) | async-done | bytes 655376 | tf_op jit(solution)/shard_map/reduce_scatter | solution.py:340
  1354.1 60.9 %reduce-scatter.14.cloned.1.call-done = f32[256,640]{1,0:T(8,128)} async-done(((f32[2048,640]{1,0:T(8,128)}), f32[256,640]{1,0:T(8,128)}) %reduce-scatter.14.cloned.1.call-update) | async-done | bytes 655376 | tf_op jit(solution)/shard_map/reduce_scatter | solution.py:341
  1415.1 96.4 %reduce-scatter.18.cloned.1.call-done = f32[256,1536]{1,0:T(8,128)} async-done(((f32[2048,1536]{1,0:T(8,128)}), f32[256,1536]{1,0:T(8,128)}) %reduce-scatter.18.cloned.1.call-update) | async-done | bytes 1572880 | tf_op jit(solution)/shard_map/reduce_scatter | solution.py:351
  1511.4 96.3 %reduce-scatter.20.cloned.1.call-done = f32[256,1536]{1,0:T(8,128)} async-done(((f32[2048,1536]{1,0:T(8,128)}), f32[256,1536]{1,0:T(8,128)}) %reduce-scatter.20.cloned.1.call-update) | async-done | bytes 1572880 | tf_op jit(solution)/shard_map/reduce_scatter | solution.py:352
  1607.8 96.4 %reduce-scatter.22.cloned.1.call-done = f32[256,1536]{1,0:T(8,128)} async-done(((f32[2048,1536]{1,0:T(8,128)}), f32[256,1536]{1,0:T(8,128)}) %reduce-scatter.22.cloned.1.call-update) | async-done | bytes 1572880 | tf_op jit(solution)/shard_map/reduce_scatter | solution.py:353
  (467 shorter events, 383.7 us)
Async XLA Ops:
  7.2 84.1 %all-gather.15.cloned.1.call-start = ((), (), s32[]{:S(2)}) async-start(), calls=%async_computation.7 | async-start | bytes 2949120 | tf_op jit(solution)/shard_map/all_gather | solution.py:158
  7.9 236.8 %all-gather.13.cloned.1.call-start = ((), (), s32[]{:S(2)}) async-start(), calls=%async_computation.6 | async-start | bytes 2949120 | tf_op jit(solution)/shard_map/all_gather | solution.py:157
  8.7 241.8 %all-gather.17.cloned.1.call-start = ((), (), s32[]{:S(2)}) async-start(), calls=%async_computation.8 | async-start | bytes 2949120 | tf_op jit(solution)/shard_map/all_gather | solution.py:166
  9.4 401.5 %all-reduce.71.cloned.1.call-start = ((), (), s32[]{:S(2)}) async-start(), calls=%async_computation.9 | async-start | bytes 8388608 | tf_op jit(solution)/shard_map/psum | solution.py:228
  10.1 23.4 %copy-start.77 = (bf16[4,20]{1,0:T(4,128)(2,1)S(1)}, bf16[4,20]{1,0:T(4,128)(2,1)}, u32[]{:S(2)}) copy-start(bf16[4,20]{1,0:T(4,128)(2,1)} %param.29) | copy-start | bytes 484
  10.1 31.3 %copy-start.48 = (bf16[4,20,160]{2,0,1:T(4,128)(2,1)S(1)}, bf16[4,20,160]{2,0,1:T(4,128)(2,1)}, u32[]{:S(2)}) copy-start(bf16[4,20,160]{2,0,1:T(4,128)(2,1)} %param.32) | copy-start | bytes 76804
  12.2 38.8 %copy-start.49 = (bf16[4,20,160]{2,0,1:T(4,128)(2,1)S(1)}, bf16[4,20,160]{2,0,1:T(4,128)(2,1)}, u32[]{:S(2)}) copy-start(bf16[4,20,160]{2,0,1:T(4,128)(2,1)} %param.30) | copy-start | bytes 76804
  12.8 78.5 %copy-start.65 = (f32[512]{0:T(512)}, f32[512]{0:T(512)S(1)}, u32[]{:S(2)}) copy-start(f32[512]{0:T(512)S(1)} %fusion.113) | copy-start | bytes 6148
  23.1 68.2 %copy-start.45 = (f32[8,1,256]{2,1,0:T(1,128)}, f32[8,1,256]{2,1,0:T(1,128)S(1)}, u32[]{:S(2)}) copy-start(f32[8,1,256]{2,1,0:T(1,128)S(1)} %convert_element_type.156) | copy-start | bytes 24580
  41.4 28.0 %copy-start.79 = (bf16[4,20]{1,0:T(4,128)(2,1)S(1)}, bf16[4,20]{1,0:T(4,128)(2,1)}, u32[]{:S(2)}) copy-start(bf16[4,20]{1,0:T(4,128)(2,1)} %param.34) | copy-start | bytes 484
  41.4 37.4 %copy-start.80 = (bf16[4,20]{1,0:T(4,128)(2,1)S(1)}, bf16[4,20]{1,0:T(4,128)(2,1)}, u32[]{:S(2)}) copy-start(bf16[4,20]{1,0:T(4,128)(2,1)} %param.33) | copy-start | bytes 484
  78.8 54.1 %copy-start.42 = (f32[640]{0:T(1024)}, f32[640]{0:T(1024)S(1)}, u32[]{:S(2)}) copy-start(f32[640]{0:T(1024)S(1)} %get-tuple-element.403) | copy-start | bytes 7684
  94.9 30.5 %copy-start.7 = (f32[512,640]{1,0:T(8,128)}, f32[512,640]{1,0:T(8,128)S(1)}, u32[]{:S(2)}) copy-start(f32[512,640]{1,0:T(8,128)S(1)} %fusion.119) | copy-start | bytes 3932164
  95.5 29.8 %collective-permute-start = (f32[1,3,640]{2,1,0:T(4,128)}, f32[1,3,640]{2,1,0:T(4,128)}, u32[]{:S(2)}, u32[]{:S(2)}) collective-permute-start(f32[1,3,640]{2,1,0:T(4,128)} %slice.515), channel_id=1, source_target_pairs={{0,4},{4,8},{8,12},{1,5},{5,9},{9,13},{2,6},{6,10},{10,14},{3,7},{... | collective-permute-start | bytes 23048 | tf_op jit(solution)/shard_map/ppermute | solution.py:16
  100.0 25.4 %copy-start.52 = (f32[640]{0:T(1024)}, f32[640]{0:T(1024)S(1)}, u32[]{:S(2)}) copy-start(f32[640]{0:T(1024)S(1)} %mul.810) | copy-start | bytes 7684
  102.3 23.1 %copy-start.54 = (f32[640]{0:T(1024)}, f32[640]{0:T(1024)S(1)}, u32[]{:S(2)}) copy-start(f32[640]{0:T(1024)S(1)} %mul.813) | copy-start | bytes 7684
  256.3 201.1 %all-gather.19.cloned.1.call-start = ((), (), s32[]{:S(2)}) async-start(), calls=%async_computation.10 | async-start | bytes 7077888 | tf_op jit(solution)/shard_map/all_gather | solution.py:168
  256.9 247.9 %all-gather.21.cloned.1.call-start = ((), (), s32[]{:S(2)}) async-start(), calls=%async_computation.11 | async-start | bytes 7077888 | tf_op jit(solution)/shard_map/all_gather | solution.py:169
  257.5 295.0 %all-gather.23.cloned.1.call-start = ((), (), s32[]{:S(2)}) async-start(), calls=%async_computation.12 | async-start | bytes 7077888 | tf_op jit(solution)/shard_map/all_gather | solution.py:170
  258.3 473.1 %all-reduce.73.cloned.1.call-start = ((), (), s32[]{:S(2)}) async-start(), calls=%async_computation.13 | async-start | bytes 8388608 | tf_op jit(solution)/shard_map/psum | solution.py:291
  267.1 469.5 %copy-start.70 = (f32[512]{0:T(512)}, f32[512]{0:T(512)S(1)}, u32[]{:S(2)}) copy-start(f32[512]{0:T(512)S(1)} %fusion.111) | copy-start | bytes 6148
  576.2 368.2 %all-reduce.75.cloned.1.call-start = ((), (), s32[]{:S(2)}) async-start(), calls=%async_computation.20 | async-start | bytes 2621440
  752.4 56.4 %slice-start = ((f32[1,32,640]{2,0,1:T(1,128)}), f32[1,1,640]{2,0,1:T(1,128)S(1)}, s32[]{:S(2)}) async-start(f32[1,32,640]{2,0,1:T(1,128)} %copy-done.33), calls=%async_computation.22 | async-start | bytes 5120 | tf_op jit(solution)/shard_map/slice | solution.py:99
  880.9 5.7 collective-permute-start.1
  882.2 351.5 %all-reduce.77.cloned.1.call-start = ((), (), s32[]{:S(2)}) async-start(), calls=%async_computation.21 | async-start | bytes 16777216 | tf_op jit(solution)/shard_map/psum | solution.py:233
  890.6 403.1 %reduce-scatter.16.cloned.1.call-start = ((), (), s32[]{:S(2)}) async-start(), calls=%async_computation.16 | async-start | bytes 5898240 | tf_op jit(solution)/shard_map/reduce_scatter | solution.py:349
  898.1 456.0 %reduce-scatter.12.cloned.1.call-start = ((), (), s32[]{:S(2)}) async-start(), calls=%async_computation.14 | async-start | bytes 5898240 | tf_op jit(solution)/shard_map/reduce_scatter | solution.py:340
  904.2 510.9 %reduce-scatter.14.cloned.1.call-start = ((), (), s32[]{:S(2)}) async-start(), calls=%async_computation.15 | async-start | bytes 5898240 | tf_op jit(solution)/shard_map/reduce_scatter | solution.py:341
  909.9 601.5 %reduce-scatter.18.cloned.1.call-start = ((), (), s32[]{:S(2)}) async-start(), calls=%async_computation.17 | async-start | bytes 14155776 | tf_op jit(solution)/shard_map/reduce_scatter | solution.py:351
  920.1 687.6 %reduce-scatter.20.cloned.1.call-start = ((), (), s32[]{:S(2)}) async-start(), calls=%async_computation.18 | async-start | bytes 14155776 | tf_op jit(solution)/shard_map/reduce_scatter | solution.py:352
  930.5 773.6 %reduce-scatter.22.cloned.1.call-start = ((), (), s32[]{:S(2)}) async-start(), calls=%async_computation.19 | async-start | bytes 14155776 | tf_op jit(solution)/shard_map/reduce_scatter | solution.py:353
  1233.7 32.6 %copy-start.69 = (f32[512]{0:T(512)S(1)}, f32[512]{0:T(512)}, u32[]{:S(2)}) copy-start(f32[512]{0:T(512)} %copy-done.68) | copy-start | bytes 6148
  (78 other events, 390.5 us)
Sparse Core Ops, SparseCore 0:
  9.9 32.8 all-gather.14
  44.7 31.4 all-gather.12
  78.0 30.1 all-gather.16
  256.4 154.4 all-reduce.70
  412.8 44.5 all-gather.18
  459.3 45.5 all-gather.20
  506.9 45.5 all-gather.22
  576.3 154.9 all-reduce.72
  882.4 57.9 all-reduce.74
  943.0 290.7 all-reduce.76
  1238.1 55.5 reduce-scatter.15
  1297.5 56.5 reduce-scatter.11
  1358.5 56.5 reduce-scatter.13
  1419.0 92.3 reduce-scatter.17
  1515.3 92.3 reduce-scatter.19
  1611.7 92.3 reduce-scatter.21
where the time goes:
time: 1720 us; the launch traced here: 1710 us
  waiting for transfers between devices  1120 us (65%)
  local copies, waits for them, and re-layouts  174 us (10%)
  matrix products  156 us (9%)
  blocking collectives  125 us (7%)
  other arithmetic  116 us (7%)
  between operations  17.5 us (1%)
    psum x1, waiting for transfers between devices, local(): lax.psum(dot_rows(hidden_low, w_down), 'tp')  286 us
    psum x1, waiting for transfers between devices, local(): middle = tok_rows + lax.psum(dot_rows(mixed_low, w_out), 'tp')  144 us
    psum x1, waiting for transfers between devices, local(): grad_normed_two = lax.psum(two_partial, 'tp')  136 us
    reduce_scatter x1, waiting for transfers between devices, local(): lax.psum_scatter(grad_w_gate, ('shard', 'ctx'), scatter_dimension=0, tile...  96.4 us
    reduce_scatter x1, waiting for transfers between devices, local(): lax.psum_scatter(grad_w_down, ('shard', 'ctx'), scatter_dimension=0, tile...  96.4 us
    reduce_scatter x1, waiting for transfers between devices, local(): lax.psum_scatter(grad_w_up, ('shard', 'ctx'), scatter_dimension=0, tiled=...  96.3 us
    reduce_scatter x1, waiting for transfers between devices, local(): lax.psum_scatter(grad_w_rec, ('shard', 'ctx'), scatter_dimension=0, tiled...  60.9 us
    reduce_scatter x1, waiting for transfers between devices, local(): lax.psum_scatter(grad_w_branch, ('shard', 'ctx'), scatter_dimension=0, ti...  60.4 us
  transfers between devices with their start and end apart: 18, of which 12 were waited for; matrix products, arithmetic and copies ran while one was open for 16% of the time, Pallas kernels for 0%

commit v1 on v0

v1 whole, which is shorter than its diff:
```python
import functools

import jax
import jax.numpy as jnp
from jax import lax
from jax.experimental import pallas as pl
from jax.experimental.pallas import tpu as pltpu
from jax.sharding import PartitionSpec as P

EPS = 1e-06
DECAY_SCALE = 8.0
F32 = jnp.float32
BF16 = jnp.bfloat16
MESH = pl.DeviceIdType.MESH
ANY = pl.BlockSpec(memory_space=pl.ANY)
VM = pl.BlockSpec(memory_space=pltpu.VMEM)
VMEM_LIMIT = 60 * 1024 * 1024


def dot(a, b):
    return jnp.dot(a, b, preferred_element_type=F32)


def dot_rows(a, b):
    return lax.dot_general(a, b, (((1,), (1,)), ((), ())), preferred_element_type=F32)


def dot_tokens(a, b):
    return lax.dot_general(a, b, (((0,), (0,)), ((), ())), preferred_element_type=F32)


def halves(v):
    hi = v.astype(BF16)
    return hi, (v - hi.astype(F32)).astype(BF16)


def gelu(v):
    return jax.nn.gelu(v)


def gelu_both(v):
    c = 0.7978845608028654
    th = jnp.tanh(c * (v + 0.044715 * v * v * v))
    half = 0.5 * (1.0 + th)
    return v * half, half + 0.5 * v * (1.0 - th * th) * c * (1.0 + 3 * 0.044715 * v * v)


def sigmoid(v):
    return 1.0 / (1.0 + jnp.exp(-v))


def minus_expm1(v):
    near = -v * (1.0 + v / 2 * (1.0 + v / 3 * (1.0 + v / 4 * (1.0 + v / 5 * (1.0 + v / 6)))))
    return jnp.where(v > -0.25, near, 1.0 - jnp.exp(v))


class Grid:
    def __init__(self, mesh):
        self.S, self.Q, self.T = (mesh.shape[n] for n in ("shard", "ctx", "tp"))
        dev = mesh.devices

        def chip(d):
            return tuple(getattr(d, "coords", None) or ())

        def paired(one, two):
            return bool(chip(one)) and chip(one) == chip(two)

        self.core_in = None
        if self.Q % 2 == 0 and paired(dev[0, 0, 0], dev[0, 1, 0]):
            self.core_in = "ctx"
        elif self.S % 2 == 0 and paired(dev[0, 0, 0], dev[1, 0, 0]):
            self.core_in = "shard"
        self.C = 1 if self.core_in is None else 2
        self.A = self.S // 2 if self.core_in == "shard" else self.S
        self.B = self.Q // 2 if self.core_in == "ctx" else self.Q
        self.N = self.S * self.Q

    def me(self):
        s, q = lax.axis_index("shard"), lax.axis_index("ctx")
        if self.core_in == "ctx":
            return s, q // 2, q % 2
        if self.core_in == "shard":
            return s // 2, q, s % 2
        return s, q, 0

    def shard_ctx(self, a, b, c):
        if self.core_in == "ctx":
            return a, b * 2 + c
        if self.core_in == "shard":
            return a * 2 + c, b
        return a, b

    def block(self, a, b, c):
        s, q = self.shard_ctx(a, b, c)
        return s * self.Q + q

    def dev(self, a, b, c):
        s, q = self.shard_ctx(a, b, c)
        return {"shard": s, "ctx": q}


class Wire:
    def __init__(self, send, recv, base=0):
        self.send, self.recv, self.used = send, recv, base

    def copy(self, src, dst, dev):
        self.used += 1
        return self.at(self.used - 1, src, dst, dev)

    def at(self, k, src, dst, dev):
        return pltpu.make_async_remote_copy(
            src_ref=src,
            dst_ref=dst,
            send_sem=self.send.at[k],
            recv_sem=self.recv.at[k],
            device_id=dev,
            device_id_type=MESH,
        )


def greet(devs):
    bar = pltpu.get_barrier_semaphore()
    for d in devs:
        pl.semaphore_signal(bar, inc=1, device_id=d, device_id_type=MESH)
    pl.semaphore_wait(bar, len(devs))


def ring_peers(size, at, place):
    if size == 1:
        return []
    if size == 2:
        return [place((at + 1) % 2)]
    return [place((at + 1) % size), place((at + size - 1) % size)]


def plane_peers(g):
    a, b, c = g.me()
    out = ring_peers(g.A, a, lambda k: g.dev(k, b, c))
    out += ring_peers(g.B, b, lambda k: g.dev(a, k, c))
    if g.C == 2:
        out.append(g.dev(a, b, 1 - c))
    return out


def gather_count(g):
    ring = 0
    for nf, ng in ((g.A, g.B), (g.B, g.A)):
        ring += (nf - 1) + (ng - 1) * nf
    return ring + (g.C - 1) * (1 + ring)


def gather_steps(g, wire, srcs, dsts):
    a, b, c = g.me()
    sib = None if g.C == 1 else g.dev(a, b, 1 - c)
    sends, sib_copies = [], []

    def ring(h):
        if h == 0:
            return g.A, a, (lambda k: g.dev(k, b, c)), g.B, b, (lambda k: g.dev(a, k, c)), (lambda f, s: g.block(f, s, c))
        return g.B, b, (lambda k: g.dev(a, k, c)), g.A, a, (lambda k: g.dev(k, b, c)), (lambda f, s: g.block(s, f, c))

    def start(src, dst, dev):
        cp = wire.copy(src, dst, dev)
        cp.start()
        sends.append(cp)
        return cp

    def rows_of(dst, blk, h, rows):
        half = rows // 2
        return dst.at[pl.ds(pl.multiple_of(blk * rows + h * half, half), half)]

    state = []
    mine = g.block(a, b, c)
    for src, dst in zip(srcs, dsts):
        rows = src.shape[0]
        half = rows // 2
        per = []
        for h in (0, 1):
            nf, f, fdev, ng, s, sdev, blk = ring(h)
            own = src.at[pl.ds(h * half, half)]
            land = rows_of(dst, mine, h, rows)
            first = start(own, land, fdev((f + 1) % nf)) if nf > 1 else None
            per.append([first, None, own, land])
        for h in (0, 1):
            nf, f, fdev, ng, s, sdev, blk = ring(h)
            _, _, own, land = per[h]
            second = {}
            if ng > 1:
                second[(0, 0)] = start(own, land, sdev((s + 1) % ng))
            per[h][1] = second
        if sib is not None:
            whole = dst.at[pl.ds(pl.multiple_of(mine * rows, rows), rows)]
            sib_copies.append(start(src, whole, sib))
        state.append(per)
        yield
    for (src, dst), per in zip(zip(srcs, dsts), state):
        rows = src.shape[0]
        for h in (0, 1):
            nf, f, fdev, ng, s, sdev, blk = ring(h)
            cp = per[h][0]
            for i in range(1, nf):
                cp.wait_recv()
                at = rows_of(dst, blk((f - i) % nf, s), h, rows)
                if i < nf - 1:
                    cp = start(at, at, fdev((f + 1) % nf))
                if ng > 1:
                    per[h][1][(0, i)] = start(at, at, sdev((s + 1) % ng))
                if sib is not None:
                    sib_copies.append(start(at, at, sib))
        yield
    for (src, dst), per in zip(zip(srcs, dsts), state):
        rows = src.shape[0]
        for h in (0, 1):
            nf, f, fdev, ng, s, sdev, blk = ring(h)
            second = per[h][1]
            for j in range(1, ng):
                for i in range(nf):
                    second[(j - 1, i)].wait_recv()
                    at = rows_of(dst, blk((f - i) % nf, (s - j) % ng), h, rows)
                    if j < ng - 1:
                        second[(j, i)] = start(at, at, sdev((s + 1) % ng))
                    if sib is not None:
                        sib_copies.append(start(at, at, sib))
        yield
    for cp in sib_copies:
        cp.wait_recv()
    for cp in sends:
        cp.wait_send()


def gather_kernel(g, n, *refs):
    srcs, dsts = refs[:n], refs[n : 2 * n]
    send, recv, here = refs[2 * n :]
    greet(plane_peers(g))
    mine = g.block(*g.me())
    locals_ = []
    for k, (src, dst) in enumerate(zip(srcs, dsts)):
        rows = src.shape[0]
        cp = pltpu.make_async_copy(src, dst.at[pl.ds(pl.multiple_of(mine * rows, rows), rows)], here.at[k])
        cp.start()
        locals_.append(cp)
    for _ in gather_steps(g, Wire(send, recv), srcs, dsts):
        pass
    for cp in locals_:
        cp.wait()


def gather_call(g, srcs, cid):
    n = len(srcs)
    count = n * gather_count(g)
    return pl.pallas_call(
        functools.partial(gather_kernel, g, n),
        out_shape=[jax.ShapeDtypeStruct((g.N * s.shape[0], s.shape[1]), s.dtype) for s in srcs],
        in_specs=[ANY] * n,
        out_specs=[ANY] * n,
        scratch_shapes=[
            pltpu.SemaphoreType.DMA((count,)),
            pltpu.SemaphoreType.DMA((count,)),
            pltpu.SemaphoreType.DMA((n,)),
        ],
        compiler_params=pltpu.CompilerParams(collective_id=cid, has_side_effects=True),
        name="gather",
    )(*srcs)


def tp_peers(g):
    t = lax.axis_index("tp")
    return ring_peers(g.T, t, lambda k: {"tp": k})


def tp_count(g, subs):
    return 2 * (g.T - 1) * subs


def tp_sum_steps(g, wire, subs, rows, partial, finish, term, sendbuf, recvbuf, out):
    T = g.T
    t = lax.axis_index("tp")
    right = {"tp": (t + 1) % T}
    sub = rows // subs
    sends = []
    last = [None] * subs
    for i in range(T):
        k = (t + 2 * T - 1 - i) % T
        partial(pl.multiple_of(k * rows, rows), rows, term)
        for u in range(subs):
            part = term[u * sub : (u + 1) * sub]
            if i > 0:
                last[u].wait_recv()
                part = part + recvbuf[i - 1, u * sub : (u + 1) * sub].astype(F32)
            if i < T - 1:
                sendbuf[i, u * sub : (u + 1) * sub] = part.astype(BF16)
                cp = wire.copy(
                    sendbuf.at[i, pl.ds(u * sub, sub)], recvbuf.at[i, pl.ds(u * sub, sub)], right
                )
                cp.start()
                sends.append(cp)
                last[u] = cp
            else:
                at = pl.multiple_of(k * rows + u * sub, sub)
                out[pl.ds(at, sub)] = finish(part, u * sub, at, sub)
                if T > 1:
                    cp = wire.copy(out.at[pl.ds(at, sub)], out.at[pl.ds(at, sub)], right)
                    cp.start()
                    sends.append(cp)
                    last[u] = cp
        yield
    for i in range(1, T):
        k = (t + T - i) % T
        for u in range(subs):
            last[u].wait_recv()
            if i < T - 1:
                at = pl.multiple_of(k * rows + u * sub, sub)
                cp = wire.copy(out.at[pl.ds(at, sub)], out.at[pl.ds(at, sub)], right)
                cp.start()
                sends.append(cp)
                last[u] = cp
        yield
    for cp in sends:
        cp.wait_send()


def tp_scratch(g, rows, width, subs):
    n = max(1, g.T - 1)
    return [
        pltpu.VMEM((rows, width), F32),
        pltpu.VMEM((n, rows, width), BF16),
        pltpu.VMEM((n, rows, width), BF16),
        pltpu.SemaphoreType.DMA((max(1, tp_count(g, subs)),)),
        pltpu.SemaphoreType.DMA((max(1, tp_count(g, subs)),)),
    ]


SUBS = 4


def tp_call(g, body, operands, out_shape, rows, width, cid, name):
    n_in, n_out = len(operands), len(out_shape)

    def kernel(*refs):
        ins, outs = refs[:n_in], refs[n_in : n_in + n_out]
        term, sendbuf, recvbuf, send, recv = refs[n_in + n_out :]
        greet(tp_peers(g))
        partial, finish = body(ins, outs)
        for _ in tp_sum_steps(g, Wire(send, recv), SUBS, rows, partial, finish, term, sendbuf, recvbuf, outs[0]):
            pass

    return pl.pallas_call(
        kernel,
        out_shape=out_shape,
        in_specs=[VM] * n_in,
        out_specs=[VM] * n_out,
        scratch_shapes=tp_scratch(g, rows, width, SUBS),
        compiler_params=pltpu.CompilerParams(
            collective_id=cid, has_side_effects=True, vmem_limit_bytes=VMEM_LIMIT
        ),
        name=name,
    )(*operands)


def tile_of(width):
    return 512 if width % 512 == 0 else width


def rows_product(term, at, n, pairs):
    width = term.shape[1]
    tile = tile_of(width)

    def body(j, _):
        c0 = pl.multiple_of(j * tile, tile)
        total = None
        for l, r in pairs:
            p = dot_rows(l[pl.ds(at, n)], r[pl.ds(c0, tile)])
            total = p if total is None else total + p
        term[:, pl.ds(c0, tile)] = total
        return 0

    lax.fori_loop(0, width // tile, body, 0)


def mean_square(v):
    return jnp.mean(v * v, axis=-1, keepdims=True)


def mix_out_body(ins, outs):
    mixed, w_out, x, gain = ins
    _, middle = outs

    def partial(at, n, term):
        rows_product(term, at, n, [(mixed, w_out)])

    def finish(total, near, at, n):
        m = x[pl.ds(at, n)].astype(F32) + total
        middle[near : near + n] = m
        return (m * lax.rsqrt(mean_square(m) + EPS) * gain[...]).astype(BF16)

    return partial, finish


def mlp_out_body(ins, outs):
    hidden, w_down, middle, live = ins

    def partial(at, n, term):
        rows_product(term, at, n, [(hidden, w_down)])

    def finish(total, near, at, n):
        return ((middle[near : near + n] + total) * live[pl.ds(at, n)]).astype(BF16)

    return partial, finish


def norm_back(grad_normed, rows, gain):
    inv = lax.rsqrt(mean_square(rows) + EPS)
    gg = grad_normed * gain
    back = inv * gg - rows * (inv * inv * inv) * jnp.mean(gg * rows, axis=-1, keepdims=True)
    return back, jnp.sum(grad_normed * rows * inv, axis=0, keepdims=True)


def mlp_back_body(ins, outs):
    gate_low, up_low, w_gate, w_up, middle, cot, live, gain = ins
    _, grad_middle, grad_gain = outs

    def partial(at, n, term):
        rows_product(term, at, n, [(gate_low, w_gate), (up_low, w_up)])

    def finish(total, near, at, n):
        back, gain_sum = norm_back(total, middle[near : near + n], gain[...])
        gm = cot[pl.ds(at, n)].astype(F32) * live[pl.ds(at, n)] + back
        grad_middle[near : near + n] = gm
        grad_gain[...] = gain_sum if near == 0 else grad_gain[...] + gain_sum
        return gm.astype(BF16)

    return partial, finish


def rec_back_body(ins, outs):
    branch_low, rec_low, w_branch, w_rec, x, grad_middle, gain = ins
    _, grad_gain = outs

    def partial(at, n, term):
        rows_product(term, at, n, [(branch_low, w_branch), (rec_low, w_rec)])

    def finish(total, near, at, n):
        back, gain_sum = norm_back(total, x[pl.ds(at, n)].astype(F32), gain[...])
        grad_gain[...] = gain_sum if near == 0 else grad_gain[...] + gain_sum
        return (grad_middle[near : near + n] + back).astype(BF16)

    return partial, finish


TAPS, SHIFT, RBIAS, EBIAS, SOFT = 0, 4, 5, 6, 7
ROWS = 64
GROUP = 8


def ctx_peers(g):
    q = lax.axis_index("ctx")
    return [{"ctx": (q + k) % g.Q} for k in range(1, g.Q)]


def swap_edges(g, wire, src, land):
    q = lax.axis_index("ctx")
    cps = []
    for k in range(1, g.Q):
        cp = wire.copy(src, land.at[q], {"ctx": (q + k) % g.Q})
        cp.start()
        cps.append(cp)
    for cp in cps:
        cp.wait_recv()
    for cp in cps:
        cp.wait_send()


def row_shift(v, n):
    return pltpu.roll(v, n % v.shape[0], 0)


def forward_kernel(g, rec, branch, w_rate, w_entry, vecs, mixed, conv, rate, entry, state, edge,
                   ext, acum, bcum, tot, halo, gath, send, recv):
    L, CH = rec.shape
    q = lax.axis_index("ctx")
    greet(ctx_peers(g))
    wire = Wire(send, recv)
    ext[8:] = rec[...]
    if g.Q > 1:
        cp = wire.copy(ext.at[pl.ds(L, 8)], halo, {"ctx": (q + 1) % g.Q})
        cp.start()
        cp.wait()
        ext[0:8] = jnp.where(q > 0, halo[...], 0.0)
    else:
        ext[0:8] = jnp.zeros((8, CH), F32)
    sub = lax.broadcasted_iota(jnp.int32, (GROUP, 1), 0)

    def chunk(i, carry):
        ca, cb = carry
        r0 = pl.multiple_of(i * ROWS, ROWS)
        wide = ext[pl.ds(r0, ROWS + 8)]
        c = vecs[SHIFT : SHIFT + 1] + vecs[TAPS : TAPS + 1] * wide[8:]
        for k in range(1, 4):
            c = c + vecs[TAPS + k : TAPS + k + 1] * row_shift(wide, k)[8:]
        conv[pl.ds(r0, ROWS)] = c
        hi, lo = halves(c)
        gr = sigmoid(dot(hi, w_rate[...]) + dot(lo, w_rate[...]) + vecs[RBIAS : RBIAS + 1])
        ge = sigmoid(dot(hi, w_entry[...]) + dot(lo, w_entry[...]) + vecs[EBIAS : EBIAS + 1])
        rate[pl.ds(r0, ROWS)] = gr
        entry[pl.ds(r0, ROWS)] = ge
        log = -DECAY_SCALE * gr * vecs[SOFT : SOFT + 1]
        dec = jnp.exp(log)
        drive = jnp.sqrt(minus_expm1(2.0 * log)) * ge * c
        for n in range(ROWS // GROUP):
            A = dec[n * GROUP : (n + 1) * GROUP]
            B = drive[n * GROUP : (n + 1) * GROUP]
            for step in (1, 2, 4):
                keep = sub >= step
                As = jnp.where(keep, row_shift(A, step), 1.0)
                Bs = jnp.where(keep, row_shift(B, step), 0.0)
                B = B + A * Bs
                A = A * As
            B = B + A * cb
            A = A * ca
            acum[pl.ds(r0 + n * GROUP, GROUP)] = A
            bcum[pl.ds(r0 + n * GROUP, GROUP)] = B
            ca = A[GROUP - 1 : GROUP]
            cb = B[GROUP - 1 : GROUP]
        return ca, cb

    ca, cb = lax.fori_loop(0, L // ROWS, chunk, (jnp.ones((1, CH), F32), jnp.zeros((1, CH), F32)))
    tot[0:1] = ca
    tot[1:2] = cb
    start = jnp.zeros((1, CH), F32)
    if g.Q > 1:
        swap_edges(g, wire, tot, gath)
        for d in range(g.Q - 1):
            new = gath[d, 0:1] * start + gath[d, 1:2]
            start = jnp.where(d < q, new, start)
    edge[...] = jnp.broadcast_to(start, (8, CH))

    def fix(i, _):
        r0 = pl.multiple_of(i * ROWS, ROWS)
        s = bcum[pl.ds(r0, ROWS)] + acum[pl.ds(r0, ROWS)] * start
        state[pl.ds(r0, ROWS)] = s
        mixed[pl.ds(r0, ROWS)] = (gelu_both(branch[pl.ds(r0, ROWS)])[0] * s).astype(BF16)
        return 0

    lax.fori_loop(0, L // ROWS, fix, 0)


def forward_call(g, rec, branch, w_rate, w_entry, vecs, cid):
    L, CH = rec.shape
    wide = jax.ShapeDtypeStruct((L, CH), F32)
    return pl.pallas_call(
        functools.partial(forward_kernel, g),
        out_shape=[jax.ShapeDtypeStruct((L, CH), BF16), wide, wide, wide, wide, jax.ShapeDtypeStruct((8, CH), F32)],
        in_specs=[VM] * 5,
        out_specs=[VM] * 6,
        scratch_shapes=[
            pltpu.VMEM((L + 8, CH), F32),
            pltpu.VMEM((L, CH), F32),
            pltpu.VMEM((L, CH), F32),
            pltpu.VMEM((8, CH), F32),
            pltpu.VMEM((8, CH), F32),
            pltpu.VMEM((g.Q, 8, CH), F32),
            pltpu.SemaphoreType.DMA((g.Q,)),
            pltpu.SemaphoreType.DMA((g.Q,)),
        ],
        compiler_params=pltpu.CompilerParams(
            collective_id=cid, has_side_effects=True, vmem_limit_bytes=VMEM_LIMIT
        ),
        name="rec_forward",
    )(rec, branch, w_rate, w_entry, vecs)


def backward_kernel(g, mid_low, w_out, branch, rec, conv, rate, entry, state, edge, w_rate, w_entry, vecs,
                    branch_low, rec_low, g_rate, g_entry, g_vecs,
                    sgrad, acum, bcum, gconv, conv_h, conv_l, rb_h, rb_l, eb_h, eb_l, tot, gath, halo, prevx, send, recv):
    L, CH = rec.shape
    q = lax.axis_index("ctx")
    greet(ctx_peers(g))
    wire = Wire(send, recv)
    tail = None
    if g.Q > 1:
        tail = wire.copy(rec.at[pl.ds(L - 8, 8)], prevx, {"ctx": (q + 1) % g.Q})
        tail.start()
    sub = lax.broadcasted_iota(jnp.int32, (GROUP, 1), 0)
    chunks = L // ROWS

    def chunk(j, carry):
        ua, ub = carry
        r0 = pl.multiple_of((chunks - 1 - j) * ROWS, ROWS)
        gm = dot(mid_low[pl.ds(r0, ROWS)], w_out[...])
        act, slope = gelu_both(branch[pl.ds(r0, ROWS)])
        branch_low[pl.ds(r0, ROWS)] = (gm * state[pl.ds(r0, ROWS)] * slope).astype(BF16)
        sg = gm * act
        sgrad[pl.ds(r0, ROWS)] = sg
        dec = jnp.exp(-DECAY_SCALE * rate[pl.ds(r0, ROWS)] * vecs[SOFT : SOFT + 1])
        sg = dec * sg
        for n in reversed(range(ROWS // GROUP)):
            A = dec[n * GROUP : (n + 1) * GROUP]
            B = sg[n * GROUP : (n + 1) * GROUP]
            for step in (1, 2, 4):
                keep = sub < GROUP - step
                As = jnp.where(keep, row_shift(A, -step), 1.0)
                Bs = jnp.where(keep, row_shift(B, -step), 0.0)
                B = B + A * Bs
                A = A * As
            B = B + A * ub
            A = A * ua
            acum[pl.ds(r0 + n * GROUP, GROUP)] = A
            bcum[pl.ds(r0 + n * GROUP, GROUP)] = B
            ua = A[0:1]
            ub = B[0:1]
        return ua, ub

    ua, ub = lax.fori_loop(0, chunks, chunk, (jnp.ones((1, CH), F32), jnp.zeros((1, CH), F32)))
    tot[0:1] = ua
    tot[1:2] = ub
    arriving = jnp.zeros((1, CH), F32)
    if g.Q > 1:
        swap_edges(g, wire, tot, gath)
        for d in reversed(range(1, g.Q)):
            new = gath[d, 0:1] * arriving + gath[d, 1:2]
            arriving = jnp.where(d > q, new, arriving)
        tail.wait()
    acum[L:] = jnp.ones((8, CH), F32)
    bcum[L:] = jnp.zeros((8, CH), F32)
    zero = jnp.zeros((1, CH), F32)
    if g.Q > 1:
        prev_rows = jnp.where(q > 0, prevx[...], 0.0)
    else:
        prev_rows = jnp.zeros((8, CH), F32)

    def back(i, carry):
        gdec, gbr, gbe, gshift, gt0, gt1, gt2, gt3, last_state, last_rec = carry
        r0 = pl.multiple_of(i * ROWS, ROWS)
        aw = row_shift(acum[pl.ds(r0, ROWS + 8)], -1)[:ROWS]
        bw = row_shift(bcum[pl.ds(r0, ROWS + 8)], -1)[:ROWS]
        car = sgrad[pl.ds(r0, ROWS)] + bw + aw * arriving
        st = state[pl.ds(r0, ROWS)]
        prev = row_shift(jnp.concatenate([last_state, st], axis=0), 1)[8:]
        gr = rate[pl.ds(r0, ROWS)]
        ge = entry[pl.ds(r0, ROWS)]
        c = conv[pl.ds(r0, ROWS)]
        soft = vecs[SOFT : SOFT + 1]
        log = -DECAY_SCALE * gr * soft
        dec = jnp.exp(log)
        scale = jnp.sqrt(minus_expm1(2.0 * log))
        ec = ge * c
        glog = car * prev * dec - car * ec * dec * dec / scale
        glr = 8.0 * glog * gr
        gdec = gdec + jnp.sum(glr, axis=0, keepdims=True)
        rb = -glr * soft * (1.0 - gr)
        cs = car * scale
        eb = cs * ec * (1.0 - ge)
        gbr = gbr + jnp.sum(rb, axis=0, keepdims=True)
        gbe = gbe + jnp.sum(eb, axis=0, keepdims=True)
        rh, rl = halves(rb)
        eh, el = halves(eb)
        ch, cl = halves(c)
        rb_h[pl.ds(r0, ROWS)] = rh
        rb_l[pl.ds(r0, ROWS)] = rl
        eb_h[pl.ds(r0, ROWS)] = eh
        eb_l[pl.ds(r0, ROWS)] = el
        conv_h[pl.ds(r0, ROWS)] = ch
        conv_l[pl.ds(r0, ROWS)] = cl
        wr, we = w_rate[...], w_entry[...]
        gc = cs * ge + dot_rows(rh, wr) + dot_rows(rl, wr) + dot_rows(eh, we) + dot_rows(el, we)
        gconv[pl.ds(r0, ROWS)] = gc
        gshift = gshift + jnp.sum(gc, axis=0, keepdims=True)
        x = rec[pl.ds(r0, ROWS)]
        wide = jnp.concatenate([last_rec, x], axis=0)
        gts = [gt0, gt1, gt2, gt3]
        for k in range(4):
            xk = x if k == 0 else row_shift(wide, k)[8:]
            gts[k] = gts[k] + jnp.sum(gc * xk, axis=0, keepdims=True)
        return (gdec, gbr, gbe, gshift, *gts, st[ROWS - 8 :], x[ROWS - 8 :])

    carry = lax.fori_loop(0, chunks, back, (zero,) * 8 + (edge[...], prev_rows))
    gdec, gbr, gbe, gshift, gt0, gt1, gt2, gt3 = carry[:8]
    if g.Q > 1:
        cp = wire.copy(gconv.at[pl.ds(0, 8)], halo, {"ctx": (q + g.Q - 1) % g.Q})
        cp.start()
    for k, v in enumerate((gt0, gt1, gt2, gt3, gshift, gbr, gbe, gdec)):
        g_vecs[k : k + 1] = v

    def product(h, l):
        return dot_tokens(conv_h[...], h[...]) + dot_tokens(conv_l[...], h[...]) + dot_tokens(conv_h[...], l[...])

    g_rate[...] = product(rb_h, rb_l)
    g_entry[...] = product(eb_h, eb_l)
    if g.Q > 1:
        cp.wait()
        gconv[L:] = jnp.where(q < g.Q - 1, halo[...], 0.0)
    else:
        gconv[L:] = jnp.zeros((8, CH), F32)

    def last(i, _):
        r0 = pl.multiple_of(i * ROWS, ROWS)
        wide = gconv[pl.ds(r0, ROWS + 8)]
        total = vecs[TAPS : TAPS + 1] * wide[:ROWS]
        for k in range(1, 4):
            total = total + vecs[TAPS + k : TAPS + k + 1] * row_shift(wide, -k)[:ROWS]
        rec_low[pl.ds(r0, ROWS)] = total.astype(BF16)
        return 0

    lax.fori_loop(0, chunks, last, 0)


def backward_call(g, mid_low, w_out, branch, rec, conv, rate, entry, state, edge, w_rate, w_entry, vecs, cid):
    L, CH = rec.shape
    low = jax.ShapeDtypeStruct((L, CH), BF16)
    dense = jax.ShapeDtypeStruct((CH, CH), F32)
    return pl.pallas_call(
        functools.partial(backward_kernel, g),
        out_shape=[low, low, dense, dense, jax.ShapeDtypeStruct((8, CH), F32)],
        in_specs=[VM] * 12,
        out_specs=[VM] * 5,
        scratch_shapes=[
            pltpu.VMEM((L, CH), F32),
            pltpu.VMEM((L + 8, CH), F32),
            pltpu.VMEM((L + 8, CH), F32),
            pltpu.VMEM((L + 8, CH), F32),
        ]
        + [pltpu.VMEM((L, CH), BF16)] * 6
        + [
            pltpu.VMEM((8, CH), F32),
            pltpu.VMEM((g.Q, 8, CH), F32),
            pltpu.VMEM((8, CH), F32),
            pltpu.VMEM((8, CH), F32),
            pltpu.SemaphoreType.DMA((g.Q + 1,)),
            pltpu.SemaphoreType.DMA((g.Q + 1,)),
        ],
        compiler_params=pltpu.CompilerParams(
            collective_id=cid, has_side_effects=True, vmem_limit_bytes=VMEM_LIMIT
        ),
        name="rec_backward",
    )(mid_low, w_out, branch, rec, conv, rate, entry, state, edge, w_rate, w_entry, vecs)


def reduce_count(g):
    ring = 0
    for nf, ng in ((g.A, g.B), (g.B, g.A)):
        ring += (nf - 1) * ng + (ng - 1)
    return ring + (g.C - 1) * g.A * g.B


def reduce_bufs(g, rows, width):
    nb = g.A * g.B
    arrivals = reduce_count(g) - (g.C - 1) * nb
    return [
        pltpu.VMEM((nb, rows, width), BF16),
        pltpu.VMEM((nb, rows, width), BF16),
        pltpu.VMEM((max(1, arrivals), rows // 2, width), BF16),
    ]


def reduce_steps(g, wire, items):
    a, b, c = g.me()
    sends = []

    def start(src, dst, dev):
        cp = wire.copy(src, dst, dev)
        cp.start()
        sends.append(cp)
        return cp

    nb = g.A * g.B

    def owner(k, core):
        return g.block((a + g.A - k // g.B) % g.A, (b + g.B - k % g.B) % g.B, core)

    def each_tile(width, fn):
        tile = tile_of(width)
        lax.fori_loop(0, width // tile, lambda j, _: fn(pl.ds(pl.multiple_of(j * tile, tile), tile)) or 0, 0)

    bases = []
    for term, out, (to_sib, sums, land) in items:
        base = wire.used
        bases.append(base)
        if g.C == 2:
            wire.used += nb

            def one(i, _):
                k = (i + 1) % nb

                def tile(cols):
                    to_sib[k, :, cols] = term(owner(k, 1 - c), cols).astype(BF16)

                each_tile(out.shape[1], tile)
                wire.at(base + k, to_sib.at[k], sums.at[k], g.dev(a, b, 1 - c)).start()
                return 0

            lax.fori_loop(0, nb, one, 0)
        yield

    rings = [(g.A, g.B), (g.B, g.A)]
    devs = [
        (g.dev((a + 1) % g.A, b, c), g.dev(a, (b + 1) % g.B, c)),
        (g.dev(a, (b + 1) % g.B, c), g.dev((a + 1) % g.A, b, c)),
    ]

    def slot(h, df, dg):
        return df * g.B + dg if h == 0 else dg * g.B + df

    state = []
    for (term, out, (to_sib, sums, land)), base in zip(items, bases):
        half = out.shape[0] // 2

        def got(k):
            if g.C == 2:
                wire.at(base + k, to_sib.at[k], sums.at[k], g.dev(a, b, 1 - c)).wait_recv()

        def one(k, _):
            got(k)

            def tile(cols):
                s = term(owner(k, c), cols)
                if g.C == 2:
                    s = s + sums[k, :, cols].astype(F32)
                sums[k, :, cols] = s.astype(BF16)

            each_tile(out.shape[1], tile)
            return 0

        lax.fori_loop(1, nb, one, 0)
        used = 0
        first = ({}, {})
        for h in (0, 1):
            nf, ng = rings[h]
            if nf > 1:
                for dg in [d % ng for d in range(1, ng + 1)]:
                    k = slot(h, 1, dg)
                    first[h][dg] = (start(sums.at[k, pl.ds(h * half, half)], land.at[used], devs[h][0]), used)
                    used += 1
        got(0)

        def tile(cols):
            s = term(owner(0, c), cols)
            if g.C == 2:
                s = s + sums[0, :, cols].astype(F32)
            out[:, cols] = s

        each_tile(out.shape[1], tile)
        state.append([first, used])
        yield

    def add(out, sums, k, h, half, arrived):
        at = slice(h * half, (h + 1) * half)
        if k == 0:
            out[at] = out[at] + arrived.astype(F32)
        else:
            sums[k, at] = (sums[k, at].astype(F32) + arrived.astype(F32)).astype(BF16)

    seconds = []
    for (term, out, (to_sib, sums, land)), st in zip(items, state):
        half = out.shape[0] // 2
        first, used = st
        second = [None, None]
        for h in (0, 1):
            nf, ng = rings[h]
            for i in range(1, nf):
                df = (i + 1) % nf
                for dg in [d % ng for d in range(1, ng + 1)]:
                    cp, at = first[h][dg]
                    cp.wait_recv()
                    k = slot(h, df, dg)
                    add(out, sums, k, h, half, land[at])
                    if i < nf - 1:
                        first[h][dg] = (start(sums.at[k, pl.ds(h * half, half)], land.at[used], devs[h][0]), used)
                        used += 1
                    elif dg == 1 and ng > 1:
                        second[h] = (start(sums.at[k, pl.ds(h * half, half)], land.at[used], devs[h][1]), used)
                        used += 1
            if nf == 1 and ng > 1:
                k = slot(h, 0, 1)
                second[h] = (start(sums.at[k, pl.ds(h * half, half)], land.at[used], devs[h][1]), used)
                used += 1
        seconds.append([second, used])
        yield
    for (term, out, (to_sib, sums, land)), (second, used) in zip(items, seconds):
        half = out.shape[0] // 2
        for h in (0, 1):
            nf, ng = rings[h]
            for j in range(1, ng):
                cp, at = second[h]
                cp.wait_recv()
                k = slot(h, 0, (j + 1) % ng)
                add(out, sums, k, h, half, land[at])
                if j < ng - 1:
                    second[h] = (start(sums.at[k, pl.ds(h * half, half)], land.at[used], devs[h][1]), used)
                    used += 1
        yield
    for cp in sends:
        cp.wait_send()
    if g.C == 2:
        for (term, out, (to_sib, sums, land)), base in zip(items, bases):
            for k in range(nb):
                wire.at(base + k, to_sib.at[k], sums.at[k], g.dev(a, b, 1 - c)).wait_send()


def reduce_call(g, pairs, given, cid, name):
    ops, where, items = [], [], []

    def place(x):
        for k, o in enumerate(ops):
            if o is x:
                return k
        ops.append(x)
        return len(ops) - 1

    for l, r in pairs:
        where.append((place(l), place(r)))
        items.append((l.shape[0] // g.N, r.shape[1]))
    for v in given:
        where.append((place(v), None))
        items.append((v.shape[0] // g.N, v.shape[1]))
    n_in, n_out = len(ops), len(items)
    count = n_out * reduce_count(g)

    def kernel(*refs):
        ins, outs = refs[:n_in], refs[n_in : n_in + n_out]
        bufs = refs[n_in + n_out : n_in + 4 * n_out]
        send, recv = refs[n_in + 4 * n_out :]
        greet(plane_peers(g))

        def term_of(where, rows):
            l, r = where

            def term(block, cols):
                at = pl.ds(pl.multiple_of(block * rows, rows), rows)
                if r is None:
                    return ins[l][at, cols]
                return dot(ins[l][at], ins[r][:, cols])

            return term

        work = [
            (term_of(where[k], items[k][0]), outs[k], bufs[3 * k : 3 * k + 3]) for k in range(n_out)
        ]
        for _ in reduce_steps(g, Wire(send, recv), work):
            pass

    scratch = []
    for rows, width in items:
        scratch += reduce_bufs(g, rows, width)
    return pl.pallas_call(
        kernel,
        out_shape=[jax.ShapeDtypeStruct(s, F32) for s in items],
        in_specs=[VM] * n_in,
        out_specs=[VM] * n_out,
        scratch_shapes=scratch
        + [pltpu.SemaphoreType.DMA((count,)), pltpu.SemaphoreType.DMA((count,))],
        compiler_params=pltpu.CompilerParams(
            collective_id=cid, has_side_effects=True, vmem_limit_bytes=VMEM_LIMIT
        ),
        name=name,
    )(*ops)


def up_to(n, k):
    return -(-n // k) * k


def small_pack(parts, rows, width):
    flat = jnp.concatenate([p.reshape(-1) for p in parts])
    return jnp.pad(flat, (0, rows * width - flat.shape[0])).reshape(rows, width)


def block_dense(blocks):
    n, w = blocks.shape[0], blocks.shape[1]
    eye = jnp.eye(n, dtype=blocks.dtype)
    return (blocks[:, :, None, :] * eye[:, None, :, None]).reshape(n * w, n * w)


def local(g, inputs, lengths, cotangent, norm1_gain, branch_weight, rec_in_weight, conv_weight, conv_bias,
          rgate_weight, rgate_bias, igate_weight, igate_bias, decay_param, out_weight, norm2_gain,
          mlp_gate_weight, mlp_up_weight, mlp_down_weight):
    slots, block_len, width = inputs.shape
    L = slots * block_len
    N, T = g.N, g.T
    chunk = L // T
    heads, rb, bw = rgate_weight.shape
    ch = heads * bw
    taps = conv_weight.shape[0]
    small = [rgate_weight, igate_weight, conv_weight, conv_bias, rgate_bias, igate_bias, decay_param, norm1_gain, norm2_gain]
    sizes = [p.size for p in small]
    srows = up_to(-(-sum(sizes) // 256), 32)
    pack = small_pack(small, srows, 256)

    got = gather_call(g, [pack, branch_weight, rec_in_weight, out_weight, mlp_gate_weight, mlp_up_weight, mlp_down_weight], 0)
    packs, w_branch, w_rec, w_out, w_gate, w_up, w_down = got
    packs = packs.reshape(N, -1)
    cut, at = [], 0
    for p, s in zip(small, sizes):
        cut.append(packs[:, at : at + s].reshape((N,) + p.shape))
        at += s
    w_rate = block_dense(cut[0].transpose(1, 0, 2, 3).reshape(heads, bw, bw))
    w_entry = block_dense(cut[1].transpose(1, 0, 2, 3).reshape(heads, bw, bw))
    taps_f = cut[2].transpose(1, 2, 0, 3).reshape(taps, ch).astype(F32)

    def channels(v):
        return v.transpose(1, 0, 2).reshape(1, ch).astype(F32)

    decay_f = channels(cut[6])
    vecs = jnp.concatenate(
        [taps_f, channels(cut[3]), channels(cut[4]), channels(cut[5]), jax.nn.softplus(-decay_f)], axis=0
    )
    gain_one = cut[7].reshape(1, width).astype(F32)
    gain_two = cut[8].reshape(1, width).astype(F32)

    x_low = inputs.reshape(L, width)
    cot = cotangent.reshape(L, width)
    positions = lax.axis_index("ctx") * block_len + jnp.arange(block_len, dtype=jnp.int32)
    live = (positions[None, :] < lengths[:, None]).astype(F32).reshape(L, 1)
    t = lax.axis_index("tp")
    x_f = x_low.astype(F32)
    low_one = (x_f * lax.rsqrt(mean_square(x_f) + EPS) * gain_one).astype(BF16)
    branch_pre = dot(low_one, w_branch)
    rec_pre = dot(low_one, w_rec)
    mixed, conv, rate, entry, state, edge = forward_call(g, rec_pre, branch_pre, w_rate, w_entry, vecs, 1)

    low = jax.ShapeDtypeStruct((L, width), BF16)
    mid = jax.ShapeDtypeStruct((chunk, width), F32)
    vec = jax.ShapeDtypeStruct((1, width), F32)
    low_two, middle = tp_call(g, mix_out_body, (mixed, w_out, x_low, gain_two), [low, mid], chunk, width, 2, "mix_out")
    gate_pre = dot(low_two, w_gate)
    up_pre = dot(low_two, w_up)
    act, slope = gelu_both(gate_pre)
    hidden = (act * up_pre).astype(BF16)
    (output,) = tp_call(g, mlp_out_body, (hidden, w_down, middle, live), [low], chunk, width, 3, "mlp_out")
    grad_low = (cot.astype(F32) * live).astype(BF16)
    grad_hidden = dot(grad_low, w_down)
    gate_low = (grad_hidden * up_pre * slope).astype(BF16)
    up_low = (grad_hidden * act).astype(BF16)
    mid_low, grad_middle, part_two = tp_call(
        g, mlp_back_body, (gate_low, up_low, w_gate, w_up, middle, cot, live, gain_two), [low, mid, vec], chunk, width, 4, "mlp_back"
    )
    g_gate, g_up, g_down = reduce_call(
        g, [(low_two.T, gate_low), (low_two.T, up_low), (grad_low.T, hidden)], [], 5, "reduce_mlp"
    )
    branch_low, rec_low, d_rate, d_entry, d_vecs = backward_call(
        g, mid_low, w_out, branch_pre, rec_pre, conv, rate, entry, state, edge, w_rate, w_entry, vecs, 6
    )
    input_grad, part_one = tp_call(
        g, rec_back_body, (branch_low, rec_low, w_branch, w_rec, x_low, grad_middle, gain_one), [low, vec], chunk, width, 7, "rec_back"
    )

    eye = jnp.eye(heads, dtype=F32)[:, None, :, None]

    def diagonal(d):
        return jnp.sum(d.reshape(heads, bw, heads, bw) * eye, axis=0).reshape(N, rb * ch)

    d_gates = jnp.concatenate([diagonal(d_rate), diagonal(d_entry)], axis=1)
    d_vecs = d_vecs.at[7].multiply(jax.nn.sigmoid(-decay_f[0]))
    d_rows = d_vecs.reshape(8, heads, N, rb).transpose(2, 0, 1, 3).reshape(N, -1)
    gains = lax.psum(jnp.concatenate([part_one, part_two], axis=0), "tp").reshape(2, N, -1).transpose(1, 0, 2).reshape(N, -1)
    flat = jnp.concatenate([d_gates, d_rows, gains], axis=1)
    prows = up_to(-(-flat.shape[1] // 256), 32)
    flat = jnp.pad(flat, ((0, 0), (0, prows * 256 - flat.shape[1]))).reshape(N * prows, 256)
    g_branch, g_rec, g_out, g_small = reduce_call(
        g, [(low_one.T, branch_low), (low_one.T, rec_low), (mid_low.T, mixed)], [flat], 8, "reduce_rec"
    )
    g_small = g_small.reshape(-1)
    n = rb * ch
    g_rate = g_small[:n].reshape(rb, heads, bw).transpose(1, 0, 2)
    g_entry = g_small[n : 2 * n].reshape(rb, heads, bw).transpose(1, 0, 2)
    rest = g_small[2 * n : 2 * n + 8 * heads * rb].reshape(8, heads, rb)
    tail = g_small[2 * n + 8 * heads * rb :]
    m = width // N
    shape = (slots, block_len, width)
    return (
        output.reshape(shape), input_grad.reshape(shape), tail[:m], g_branch, g_rec, rest[:taps], rest[4],
        g_rate, rest[5], g_entry, rest[6], rest[7], g_out, tail[m : 2 * m], g_gate, g_up, g_down,
    )


def solution(mesh):
    plane = ("shard", "ctx")
    rows, cols = P(plane), P(plane, "tp")
    tok, gate, chan = P("shard", "ctx", None), P("tp", plane, None), P("tp", plane)
    taps = P(None, "tp", plane)
    params = (rows, cols, cols, taps, chan, gate, chan, gate, chan, chan, cols, rows, cols, cols, cols)
    return jax.shard_map(
        functools.partial(local, Grid(mesh)),
        mesh=mesh,
        in_specs=(tok, P("shard"), tok) + params,
        out_specs=(tok, tok) + params,
        check_vma=False,
    )
```

time: 1720 us -> 785 us (0.46)
  waiting for transfers between devices: 1120 us -> 0 us
  Pallas kernels: 0 us -> 637 us
  matrix products: 156 us -> 38.4 us
  local copies, waits for them, and re-layouts: 174 us -> 64.1 us
  blocking collectives: 125 us -> 16.1 us
  other arithmetic: 116 us -> 17.8 us
    pallas_call x0 -> x9, Pallas kernels: none -> 637 us  [the longest x4 320 us: tp_call(): pl.pallas_call(kernel, out_shape=out_shape, in_specs=[VM] * n_in, out_spe...]
    psum x3 -> x0, waiting for transfers between devices: 566 us -> none  [the longest x1 286 us: local(): lax.psum(dot_rows(hidden_low, w_down), 'tp')]
    reduce_scatter x6 -> x0, waiting for transfers between devices: 428 us -> none  [the longest x1 96.4 us: local(): lax.psum_scatter(grad_w_gate, ('shard', 'ctx'), scatter_dimension=0, tile...]
    all_gather x6 -> x0, waiting for transfers between devices: 118 us -> none  [the longest x1 39.9 us: local(): lax.all_gather(mlp_gate_weight, ('shard', 'ctx'), axis=0, tiled=True)]
    dot_general x26 -> x5, matrix products: 156 us -> 38.4 us  [dot(): return jnp.dot(a, b, preferred_element_type=F32)]
    all_gather x13 -> x0, blocking collectives: 101 us -> none  [the longest x4 20.6 us: entering(): everything = jax.tree.map(lambda part: lax.all_gather(part, axis), x)]
    pad x24 -> x1, local copies, waits for them, and re-layouts: 56.5 us -> 0.01 us  [small_pack(): return jnp.pad(flat, (0, rows * width - flat.shape[0])).reshape(rows, width)]
    add x43 -> x0, other arithmetic: 41.6 us -> none  [the longest x20 24.1 us: block_scan(): lax.associative_scan(affine_join, (part_decay, part_state), axis=1, rever...]
  transfers between devices with their start and end apart: 18 -> 0, of which waited for: 12 -> 0; matrix products, arithmetic and copies ran while one was open for 16% -> 0% of each run, Pallas kernels for 0% -> 0%
where the time goes in v1:
time: 785 us; the launch traced here: 775 us
  Pallas kernels  637 us (81%)
  local copies, waits for them, and re-layouts  64.1 us (8%)
  matrix products  38.4 us (5%)
  other arithmetic  17.8 us (2%)
  blocking collectives  16.1 us (2%)
    pallas_call x4, Pallas kernels, tp_call(): pl.pallas_call(kernel, out_shape=out_shape, in_specs=[VM] * n_in, out_spe...  320 us
    pallas_call x2, Pallas kernels, reduce_call(): pl.pallas_call(kernel, out_shape=[jax.ShapeDtypeStruct(s, F32) for s in i...  147 us
    pallas_call x1, Pallas kernels, gather_call(): pl.pallas_call(functools.partial(gather_kernel, g, n), out_shape=[jax.Sha...  119 us
    dot_general x5, matrix products, dot(): return jnp.dot(a, b, preferred_element_type=F32)  38.4 us
    pallas_call x1, Pallas kernels, backward_call(): pl.pallas_call(functools.partial(backward_kernel, g), out_shape=[low, low...  32 us
    unnamed x53, local copies, waits for them, and re-layouts  21 us
    pallas_call x1, Pallas kernels, forward_call(): pl.pallas_call(functools.partial(forward_kernel, g), out_shape=[jax.Shape...  18.2 us
    psum x1, blocking collectives, local(): lax.psum(jnp.concatenate([part_one, part_two], axis=0), 'tp')  16.1 us

profile of v1, /device:TPU:0, one launch (start us, length us, event | category | flops | bytes accessed | tf_op | source)
XLA Modules:
  0.0 775.0 jit_solution(15045788881367399294)
XLA Ops:
  6.3 1.4 concatenate.14
  8.4 119.2 %gather.1 = (bf16[1024,256]{1,0:T(8,128)(2,1)}, bf16[2048,640]{1,0:T(8,128)(2,1)}, bf16[2048,640]{1,0:T(8,128)(2,1)}, bf16[2048,640]{1,0:T(8,128)(2,1)}, bf16[20...) custom-call(bf16[128,256]{1,0:T(8,128)(2,1)} %reshape.388.refs_0_, ...), custom_call_target="tpu_custom_call" | custom-call | tf_op jit(solution)/shard_map/gather/pallas_call | solution.py:251
  127.7 1.3 reshape.389
  130.9 2.5 copy.49
  133.4 2.1 fusion
  135.5 5.6 fusion.20.branch
  141.1 3.1 fusion.22.rec
  146.3 3.4 broadcast_multiply_fusion
  149.8 2.8 mul.155.w_rate
  152.5 1.6 mul.159.w_entry
  154.1 18.2 %rec_forward.1 = (bf16[512,640]{1,0:T(8,128)(2,1)}, f32[512,640]{1,0:T(8,128)}, f32[512,640]{1,0:T(8,128)}, f32[512,640]{1,0:T(8,128)}, f32[512,640]{1,0:T(8,128)}, /*index=5*/f32[8,640]{1,0:T(8,128)}) custom-call(f32[512,640]{1,0:T(8,128)} %fusion.22.rec, f32[512,640]{1,0:T(8,128)} %fusion.20.branch, bf16[640,640]{1,0:T(8,128)(2,1)} %mul.155.w_rate, ...), custom_call_target="tpu_custom_call" | custom-call | tf_op jit(solution)/shard_map/rec_forward/pallas_call | solution.py:550
  172.9 78.3 %mix_out.1 = (bf16[512,2048]{1,0:T(8,128)(2,1)}, f32[128,2048]{1,0:T(8,128)}) custom-call(bf16[512,640]{1,0:T(8,128)(2,1)} %get-tuple-element.64.refs_0_.refs_5_, bf16[2048,640]{1,0:T(8,128)(2,1)} %get-tuple-element.65.refs_1_.w_out, bf16[512,2048]{1,0:T(8,128)(2,1)} %bitcast.82, f32[1,2048]{1,0:T(1,128)} %bitcast.102), custom_call_target="tpu_custom_call" | custom-call | tf_op jit(solution)/shard_map/mix_out/pallas_call | solution.py:347
  251.3 8.7 %fusion.29 = f32[512,1536]{1,0:T(8,128)} fusion(bf16[512,2048]{1,0:T(8,128)(2,1)} %get-tuple-element.66, bf16[2048,1536]{1,0:T(8,128)(2,1)} %get-tuple-element.68.refs_3_), kind=kOutput, calls=%fused_computation.66 | convolution fusion | flops 3221225472 | bytes 11534336 | tf_op jit(solution)/shard_map/dot_general | solution.py:21
  259.9 7.9 %fusion.28 = f32[512,1536]{1,0:T(8,128)} fusion(bf16[512,2048]{1,0:T(8,128)(2,1)S(1)} %copy-done.4, bf16[2048,1536]{1,0:T(8,128)(2,1)} %get-tuple-element.67.refs_2_), kind=kOutput, calls=%fused_computation.65 | convolution fusion | flops 3221225472 | bytes 11534336 | tf_op jit(solution)/shard_map/dot_general | solution.py:21
  268.5 3.9 copy.62
  272.5 13.2 %multiply_convert_fusion.1 = (bf16[512,1536]{1,0:T(8,128)(2,1)}, bf16[512,1536]{1,0:T(8,128)(2,1)}, bf16[512,1536]{1,0:T(8,128)(2,1)}) fusion(f32[512,1536]{1,0:T(8,128)} %fusion.28, f32[512,1536]{1,0:T(8,128)} %fusion.29, bf16[2048,1536]{1,0:T(8,128)(2,1)} %get-tuple-element.69.refs_1_, bf16[1,512,2048]{1,2,0:T(8,128)(2,1)} %copy.62, f32[512]{0:T(512)S(1)} %fusion.18), kind=kOutput, calls=%fused_computation.15 | convolution fusion | flops 3244032000 | bytes 19400704 | tf_op jit(solution)/shard_map/dot_general | solution.py:21
  285.6 3.9 copy.68
  289.5 3.3 fusion.11.refs_4_
  292.8 99.4 %reduce_mlp.1 = (f32[256,1536]{1,0:T(8,128)}, f32[256,1536]{1,0:T(8,128)}, f32[256,1536]{1,0:T(8,128)}) custom-call(bf16[2048,512]{1,0:T(8,128)(2,1)} %bitcast.84, bf16[512,1536]{1,0:T(8,128)(2,1)} %get-tuple-element.96.refs_0_.refs_1_, bf16[2048,512]{1,0:T(8,128)(2,1)} %bitcast.85, bf16[512,1536]{1,0:T(8,128)(2,1)} %get-tuple-element.95.refs_1_.refs_3_, ...), custom_call_target="tpu_custom_call" | custom-call | tf_op jit(solution)/shard_map/reduce_mlp/pallas_call | solution.py:944
  393.0 83.8 %mlp_back.1 = (bf16[512,2048]{1,0:T(8,128)(2,1)}, f32[128,2048]{1,0:T(8,128)}, f32[1,2048]{1,0:T(1,128)}) custom-call(bf16[512,1536]{1,0:T(8,128)(2,1)} %get-tuple-element.96.refs_0_.refs_1_, bf16[512,1536]{1,0:T(8,128)(2,1)} %get-tuple-element.95.refs_1_.refs_3_, bf16[2048,1536]{1,0:T(8,128)(2,1)} %get-tuple-element.67.refs_2_, ...), custom_call_target="tpu_custom_call" | custom-call | tf_op jit(solution)/shard_map/mlp_back/pallas_call | solution.py:347
  476.7 32.0 %rec_backward.1 = (bf16[512,640]{1,0:T(8,128)(2,1)}, bf16[512,640]{1,0:T(8,128)(2,1)}, f32[640,640]{1,0:T(8,128)}, f32[640,640]{1,0:T(8,128)}, f32[8,640]{1,0:T(8,128)}) custom-call(bf16[512,2048]{1,0:T(8,128)(2,1)} %get-tuple-element.71.mid_low, bf16[2048,640]{1,0:T(8,128)(2,1)} %get-tuple-element.65.refs_1_.w_out, f32[512,640]{1,0:T(8,128)} %fusion.20.branch, ...), custom_call_target="tpu_custom_call" | custom-call | tf_op jit(solution)/shard_map/rec_backward/pallas_call | solution.py:711
  508.7 4.1 reshape.395
  512.9 4.2 reshape.397
  517.1 4.3 multiply_reduce_fusion.1
  525.9 79.8 %rec_back.1 = (bf16[512,2048]{1,0:T(8,128)(2,1)}, f32[1,2048]{1,0:T(1,128)}) custom-call(bf16[512,640]{1,0:T(8,128)(2,1)} %get-tuple-element.77.refs_0_.refs_1_, bf16[512,640]{1,0:T(8,128)(2,1)} %get-tuple-element.78.refs_1_.refs_3_, bf16[2048,640]{1,0:T(8,128)(2,1)} %get-tuple-element.63.refs_2_, bf16[2048,640]{1,0:T(8,128)(2,1)} %get-tuple-element.62.refs_3_, ...), custom_call_target="tpu_custom_call" | custom-call | tf_op jit(solution)/shard_map/rec_back/pallas_call | solution.py:347
  606.5 16.1 %psum.7 = f32[8,512]{1,0:T(8,128)} all-reduce(f32[8,512]{1,0:T(8,128)S(1)} %bitcast.110), channel_id=1, replica_groups=mesh['shard'=2,'ctx'=4,'tp'=4] {'tp'}, use_global_device_ids=true, to_apply=%region_3.4 | all-reduce | flops 4096 | bytes 32768 | tf_op jit(solution)/shard_map/psum | solution.py:1054
  624.8 3.9 copy.65
  628.8 1.9 fusion.19.refs_0_.refs_2_
  630.6 47.4 %reduce_rec.1 = (f32[256,640]{1,0:T(8,128)}, f32[256,640]{1,0:T(8,128)}, f32[256,640]{1,0:T(8,128)}, f32[128,256]{1,0:T(8,128)}) custom-call(bf16[2048,512]{1,0:T(8,128)(2,1)} %fusion.19.refs_0_.refs_2_, bf16[512,640]{1,0:T(8,128)(2,1)} %get-tuple-element.77.refs_0_.refs_1_, bf16[2048,512]{1,0:T(8,128)(2,1)} %fusion.19.refs_0_.refs_2_, ...), custom_call_target="tpu_custom_call" | custom-call | tf_op jit(solution)/shard_map/reduce_rec/pallas_call | solution.py:944
  685.4 78.4 %mlp_out.1 = bf16[512,2048]{1,0:T(8,128)(2,1)} custom-call(bf16[512,1536]{1,0:T(8,128)(2,1)} %get-tuple-element.97.refs_0_.refs_5_, bf16[2048,1536]{1,0:T(8,128)(2,1)} %get-tuple-element.69.refs_1_, f32[128,2048]{1,0:T(8,128)} %get-tuple-element.70.refs_2_.refs_4_, f32[512,1]{1,0:T(8,128)} %fusion.13.refs_3_.refs_6_), custom_call_target="tpu_custom_call" | custom-call | tf_op jit(solution)/shard_map/mlp_out/pallas_call | solution.py:347
  763.8 3.3 copy.101
  767.2 1.3 copy.102
  (115 shorter events, 32.5 us)
Async XLA Ops:
  8.4 122.5 %copy-start = (bf16[1,512,2048]{2,1,0:T(8,128)(2,1)S(1)}, bf16[1,512,2048]{2,1,0:T(8,128)(2,1)}, u32[]{:S(2)}) copy-start(bf16[1,512,2048]{2,1,0:T(8,128)(2,1)} %param.20) | copy-start | bytes 6291460
  130.9 10.2 %copy-start.12 = (f32[1,2,8,128]{3,1,2,0:T(2,128)}, f32[1,2,8,128]{3,1,2,0:T(2,128)S(1)}, u32[]{:S(2)}) copy-start(f32[1,2,8,128]{3,1,2,0:T(2,128)S(1)} %copy.72) | copy-start | bytes 24580
  135.5 5.6 copy-start.15
  135.5 5.6 copy-start.1
  135.5 5.6 copy-start.2
  251.3 8.7 %copy-start.4 = (bf16[512,2048]{1,0:T(8,128)(2,1)S(1)}, bf16[512,2048]{1,0:T(8,128)(2,1)}, u32[]{:S(2)}) copy-start(bf16[512,2048]{1,0:T(8,128)(2,1)} %get-tuple-element.66) | copy-start | bytes 6291460
  517.1 7.1 copy-start.14
  525.9 79.8 %copy-start.17 = (f32[1,2048]{1,0:T(1,128)S(1)}, f32[1,2048]{1,0:T(1,128)}, u32[]{:S(2)}) copy-start(f32[1,2048]{1,0:T(1,128)} %get-tuple-element.85) | copy-start | bytes 24580
  525.9 96.7 %copy-start.5 = (f32[8,12800]{1,0:T(8,128)S(1)}, f32[8,12800]{1,0:T(8,128)}, u32[]{:S(2)}) copy-start(f32[8,12800]{1,0:T(8,128)} %reshape.396) | copy-start | bytes 1228804
  624.8 3.9 copy-start.13
  624.8 3.9 copy-start.16
  763.8 3.3 copy-start.3
  767.1 1.5 copy-start.11
  767.1 2.4 copy-start.10
  767.2 3.2 copy-start.9
  768.7 2.5 copy-start.8
  769.5 2.8 copy-start.7
  771.2 2.3 copy-start.6

commit v2 on v1

--- a/solution.py
+++ b/solution.py
@@ -14,7 +14,7 @@
 MESH = pl.DeviceIdType.MESH
 ANY = pl.BlockSpec(memory_space=pl.ANY)
 VM = pl.BlockSpec(memory_space=pltpu.VMEM)
-VMEM_LIMIT = 60 * 1024 * 1024
+VMEM_LIMIT = 63 * 1024 * 1024
 
 
 def dot(a, b):
@@ -142,6 +142,83 @@
     return out
 
 
+def braid(main, *sides):
+    k = 0
+    for _ in main:
+        for steps, plan in sides:
+            for _ in range(plan[k] if k < len(plan) else 0):
+                next(steps, None)
+        k += 1
+    left = [s[0] for s in sides]
+    while left:
+        left = [s for s in left if next(s, left) is not left]
+
+
+def at_steps(*pairs):
+    plan = [0] * (1 + max(last for _, last, _ in pairs))
+    for first, last, each in pairs:
+        for k in range(first, last + 1):
+            plan[k] += each
+    return tuple(plan)
+
+
+ALWAYS = (1,) * 64
+
+
+def run(*steps):
+    for s in steps:
+        for _ in s:
+            pass
+
+
+class Later:
+    def __init__(self, src, dst, sem):
+        self.copy, self.dst, self.here = pltpu.make_async_copy(src, dst, sem), dst, False
+        self.copy.start()
+
+    def ref(self):
+        if not self.here:
+            self.copy.wait()
+            self.here = True
+        return self.dst
+
+
+def call(kernel, operands, out_shape, scratch, cid, name, in_specs=None, out_specs=None, later=()):
+    in_specs = list(in_specs or [VM] * len(operands))
+    for k in later:
+        in_specs[k] = ANY
+    n = len(later)
+    n_in = len(operands)
+
+    def body(*refs):
+        refs = list(refs)
+        if n:
+            kept, sem = refs[-n - 1 : -1], refs[-1]
+            refs = refs[: -n - 1]
+            for j, k in enumerate(later):
+                refs[k] = Later(refs[k], kept[j], sem.at[j])
+        kernel(*refs)
+
+    extra = [pltpu.VMEM(operands[k].shape, operands[k].dtype) for k in later]
+    if n:
+        extra.append(pltpu.SemaphoreType.DMA((n,)))
+    return pl.pallas_call(
+        body,
+        out_shape=out_shape,
+        in_specs=in_specs,
+        out_specs=out_specs or [VM] * len(out_shape),
+        scratch_shapes=list(scratch) + extra,
+        compiler_params=pltpu.CompilerParams(
+            collective_id=cid, has_side_effects=True, vmem_limit_bytes=VMEM_LIMIT
+        ),
+        name=name,
+    )(*operands)
+
+
+def sems(n):
+    return [pltpu.SemaphoreType.DMA((max(1, n),)), pltpu.SemaphoreType.DMA((max(1, n),))]
+
+
 def gather_count(g):
     ring = 0
     for nf, ng in ((g.A, g.B), (g.B, g.A)):
@@ -149,7 +226,7 @@
     return ring + (g.C - 1) * (1 + ring)
 
 
-def gather_steps(g, wire, srcs, dsts):
+def gather_steps(g, wire, here, srcs, dsts):
     a, b, c = g.me()
     sib = None if g.C == 1 else g.dev(a, b, 1 - c)
     sends, sib_copies = [], []
@@ -171,9 +248,13 @@
 
     state = []
     mine = g.block(a, b, c)
+    local_copies = []
     for src, dst in zip(srcs, dsts):
         rows = src.shape[0]
         half = rows // 2
+        cp = pltpu.make_async_copy(src, dst.at[pl.ds(pl.multiple_of(mine * rows, rows), rows)], here.at[len(local_copies)])
+        cp.start()
+        local_copies.append(cp)
         per = []
         for h in (0, 1):
             nf, f, fdev, ng, s, sdev, blk = ring(h)
@@ -222,6 +303,8 @@
                     if sib is not None:
                         sib_copies.append(start(at, at, sib))
         yield
+    for cp in local_copies:
+        cp.wait()
     for cp in sib_copies:
         cp.wait_recv()
     for cp in sends:
@@ -232,17 +315,7 @@
     srcs, dsts = refs[:n], refs[n : 2 * n]
     send, recv, here = refs[2 * n :]
     greet(plane_peers(g))
-    mine = g.block(*g.me())
-    locals_ = []
-    for k, (src, dst) in enumerate(zip(srcs, dsts)):
-        rows = src.shape[0]
-        cp = pltpu.make_async_copy(src, dst.at[pl.ds(pl.multiple_of(mine * rows, rows), rows)], here.at[k])
-        cp.start()
-        locals_.append(cp)
-    for _ in gather_steps(g, Wire(send, recv), srcs, dsts):
-        pass
-    for cp in locals_:
-        cp.wait()
+    run(gather_steps(g, Wire(send, recv), here, srcs, dsts))
 
 
 def gather_call(g, srcs, cid):
@@ -251,7 +324,7 @@
     return pl.pallas_call(
         functools.partial(gather_kernel, g, n),
         out_shape=[jax.ShapeDtypeStruct((g.N * s.shape[0], s.shape[1]), s.dtype) for s in srcs],
-        in_specs=[ANY] * n,
+        in_specs=[VM] * n,
         out_specs=[ANY] * n,
         scratch_shapes=[
             pltpu.SemaphoreType.DMA((count,)),
@@ -268,93 +341,183 @@
     return ring_peers(g.T, t, lambda k: {"tp": k})
 
 
-def tp_count(g, subs):
-    return 2 * (g.T - 1) * subs
-
-
-def tp_sum_steps(g, wire, subs, rows, partial, finish, term, sendbuf, recvbuf, out):
+MIX_XY = at_steps((6, 6, 1), (12, 12, 1), (16, 16, 1), (19, 19, 1))
+BACK_Z = ALWAYS
+BACK_DOWN = at_steps((0, 7, 1), (9, 9, 1), (18, 18, 1))
+BACK_OUT = at_steps((10, 17, 1), (20, 20, 1))
+MLP_GATE = at_steps((0, 3, 2), (8, 8, 1), (14, 14, 1))
+MLP_UP = at_steps((4, 7, 2), (14, 14, 1), (21, 21, 1))
+REC_BRANCH = at_steps((0, 3, 2), (9, 9, 1), (17, 17, 1))
+REC_REC = at_steps((4, 7, 2), (13, 13, 1), (19, 19, 1))
+REC_SMALL = at_steps((8, 11, 2), (15, 15, 1), (20, 20, 1))
+PIECE = 32
+CHUNK = 256
+
+
+def tp_count(g, rows):
+    return 4 * (rows // 2 // PIECE)
+
+
+def tp_place(g):
+    t = lax.axis_index("tp")
+    side = jnp.where(t >= (g.T + 1) // 2, 1, 0)
+    return side, jnp.where(side == 1, g.T - 1 - t, t)
+
+
+END = {"send_near": 0, "take_far": 8, "take_near": 14}
+INNER = {"send_near": 0, "take_far": 2, "pass_far": 6, "take_near": 8}
+
+
+def tp_steps(g, wire, rows, out, partial=None, finish=None, bufs=None, gather=True):
     T = g.T
     t = lax.axis_index("tp")
-    right = {"tp": (t + 1) % T}
-    sub = rows // subs
-    sends = []
-    last = [None] * subs
-    for i in range(T):
-        k = (t + 2 * T - 1 - i) % T
-        partial(pl.multiple_of(k * rows, rows), rows, term)
-        for u in range(subs):
-            part = term[u * sub : (u + 1) * sub]
-            if i > 0:
-                last[u].wait_recv()
-                part = part + recvbuf[i - 1, u * sub : (u + 1) * sub].astype(F32)
-            if i < T - 1:
-                sendbuf[i, u * sub : (u + 1) * sub] = part.astype(BF16)
-                cp = wire.copy(
-                    sendbuf.at[i, pl.ds(u * sub, sub)], recvbuf.at[i, pl.ds(u * sub, sub)], right
-                )
-                cp.start()
-                sends.append(cp)
-                last[u] = cp
-            else:
-                at = pl.multiple_of(k * rows + u * sub, sub)
-                out[pl.ds(at, sub)] = finish(part, u * sub, at, sub)
-                if T > 1:
-                    cp = wire.copy(out.at[pl.ds(at, sub)], out.at[pl.ds(at, sub)], right)
-                    cp.start()
-                    sends.append(cp)
-                    last[u] = cp
+    half = rows // 2
+    pieces = half // PIECE
+    side, pos = tp_place(g)
+    end, inner = pos == 0, pos > 0
+    near, far = side, 1 - side
+    away = {"tp": jnp.where(side == 1, t - 1, t + 1)}
+    home = {"tp": jnp.where(side == 1, (t + 1) % T, (t + T - 1) % T)}
+    k_rs = wire.used
+    if partial is not None:
+        wire.used += 2 * pieces
+    k_ag = wire.used
+    if gather:
+        wire.used += 2 * pieces
+
+    def row(d, p):
+        return pl.multiple_of(half * (1 - d) + p * PIECE, PIECE)
+
+    def rs(d, p, dev):
+        return wire.at(k_rs + d * pieces + p, bufs[1].at[d, p], bufs[2].at[d, p], dev)
+
+    def ag(d, p, dev):
+        at = out.at[pl.ds(row(d, p), PIECE)]
+        return wire.at(k_ag + d * pieces + p, at, at, dev)
+
+    step = chunk_rows(g, rows, out.shape[1])
+    per = step // PIECE
+
+    def ready(d, p, which):
+        term = bufs[0].at[which]
+        if p % per == 0:
+            partial(pl.multiple_of(half * (1 - d) + p * PIECE, step), step, term)
+        return term.at[pl.ds(p % per * PIECE, PIECE)]
+
+    def send_near(p, at_end):
+        part = ready(near, p, 0)[...]
+        if not at_end:
+            rs(near, p, away).wait_recv()
+            part = part + bufs[2][near, p].astype(F32)
+        bufs[1][near, p] = part.astype(BF16)
+        rs(near, p, away).start()
+
+    def take_far(p, at_end):
+        part = ready(far, p, 1)
+        rs(far, p, home).wait_recv()
+        total = part[...] + bufs[2][far, p].astype(F32)
+        if not at_end:
+            bufs[1][far, p] = total.astype(BF16)
+            rs(far, p, home).start()
+            return
+        done = finish(total, p * PIECE, row(far, p), PIECE)
+        if gather:
+            out[pl.ds(row(far, p), PIECE)] = done
+            ag(far, p, away).start()
+        else:
+            out[p * PIECE : (p + 1) * PIECE] = done
+
+    def pass_far(p, at_end):
+        ag(far, p, away).wait_recv()
+        ag(far, p, away).start()
+
+    def take_near(p, at_end):
+        ag(near, p, home).wait_recv()
+        if not at_end:
+            ag(near, p, home).start()
+
+    acts = {"send_near": send_near, "take_far": take_far, "pass_far": pass_far, "take_near": take_near}
+    if partial is None:
+
+        @pl.when(end)
+        def _():
+            for p in range(pieces):
+                ag(far, p, away).start()
+
+        acts = {"pass_far": pass_far, "take_near": take_near}
         yield
-    for i in range(1, T):
-        k = (t + T - i) % T
-        for u in range(subs):
-            last[u].wait_recv()
-            if i < T - 1:
-                at = pl.multiple_of(k * rows + u * sub, sub)
-                cp = wire.copy(out.at[pl.ds(at, sub)], out.at[pl.ds(at, sub)], right)
-                cp.start()
-                sends.append(cp)
-                last[u] = cp
+    elif not gather:
+        acts = {"send_near": send_near, "take_far": take_far}
+
+    def schedule(lates):
+        lates = {k: v for k, v in lates.items() if k in acts}
+        least = min(lates.values())
+        return [(acts[k], v - least) for k, v in lates.items()]
+
+    plans = [(end, True, schedule(END)), (inner, False, schedule(INNER))]
+    for i in range(pieces + max(late for _, _, plan in plans for _, late in plan)):
+        for where, at_end, plan in plans:
+
+            @pl.when(where)
+            def _():
+                for act, late in plan:
+                    if 0 <= i - late < pieces:
+                        act(i - late, at_end)
+
         yield
-    for cp in sends:
-        cp.wait_send()
-
-
-def tp_scratch(g, rows, width, subs):
-    n = max(1, g.T - 1)
+    if partial is not None:
+        for p in range(pieces):
+            rs(near, p, away).wait_send()
+    if gather:
+        for p in range(pieces):
+            ag(far, p, away).wait_send()
+
+    @pl.when(inner)
+    def _():
+        for p in range(pieces):
+            if partial is not None:
+                rs(far, p, home).wait_send()
+            if gather:
+                ag(near, p, home).wait_send()
+
+
+def chunk_rows(g, rows, width):
+    return min(CHUNK // 2 if needs_turn(width // g.N) else CHUNK, rows // 2)
+
+
+def tp_bufs(g, rows, width):
+    pieces = rows // 2 // PIECE
     return [
-        pltpu.VMEM((rows, width), F32),
-        pltpu.VMEM((n, rows, width), BF16),
-        pltpu.VMEM((n, rows, width), BF16),
-        pltpu.SemaphoreType.DMA((max(1, tp_count(g, subs)),)),
-        pltpu.SemaphoreType.DMA((max(1, tp_count(g, subs)),)),
+        pltpu.VMEM((2, chunk_rows(g, rows, width), width), F32),
+        pltpu.VMEM((2, pieces, PIECE, width), BF16),
+        pltpu.VMEM((2, pieces, PIECE, width), BF16),
     ]
 
 
-SUBS = 4
-
-
-def tp_call(g, body, operands, out_shape, rows, width, cid, name):
-    n_in, n_out = len(operands), len(out_shape)
-
-    def kernel(*refs):
-        ins, outs = refs[:n_in], refs[n_in : n_in + n_out]
-        term, sendbuf, recvbuf, send, recv = refs[n_in + n_out :]
-        greet(tp_peers(g))
-        partial, finish = body(ins, outs)
-        for _ in tp_sum_steps(g, Wire(send, recv), SUBS, rows, partial, finish, term, sendbuf, recvbuf, outs[0]):
-            pass
-
-    return pl.pallas_call(
-        kernel,
-        out_shape=out_shape,
-        in_specs=[VM] * n_in,
-        out_specs=[VM] * n_out,
-        scratch_shapes=tp_scratch(g, rows, width, SUBS),
-        compiler_params=pltpu.CompilerParams(
-            collective_id=cid, has_side_effects=True, vmem_limit_bytes=VMEM_LIMIT
-        ),
-        name=name,
-    )(*operands)
+def transpose_steps(dst, src, scale=None):
+    if isinstance(src, Later):
+        src = src.ref()
+    width = src.shape[1]
+    part = 512
+    assert width % part == 0
+
+    for at in range(0, width, part):
+
+        def body(j, _):
+            c0 = pl.multiple_of(at + j * 128, 128)
+            v = src[:, pl.ds(c0, 128)]
+            if scale is not None:
+                v = (v.astype(F32) * scale[...]).astype(BF16)
+            dst[pl.ds(c0, 128), :] = v.T
+            return 0
+
+        lax.fori_loop(0, part // 128, body, 0)
+        yield
+
+
+def chain(*steps):
+    for s in steps:
+        yield from s
 
 
 def tile_of(width):
@@ -418,6 +581,7 @@
 def mlp_back_body(ins, outs):
     gate_low, up_low, w_gate, w_up, middle, cot, live, gain = ins
     _, grad_middle, grad_gain = outs
+    grad_gain[...] = jnp.zeros_like(grad_gain)
 
     def partial(at, n, term):
         rows_product(term, at, n, [(gate_low, w_gate), (up_low, w_up)])
@@ -426,7 +590,7 @@
         back, gain_sum = norm_back(total, middle[near : near + n], gain[...])
         gm = cot[pl.ds(at, n)].astype(F32) * live[pl.ds(at, n)] + back
         grad_middle[near : near + n] = gm
-        grad_gain[...] = gain_sum if near == 0 else grad_gain[...] + gain_sum
+        grad_gain[...] = grad_gain[...] + gain_sum
         return gm.astype(BF16)
 
     return partial, finish
@@ -435,19 +599,20 @@
 def rec_back_body(ins, outs):
     branch_low, rec_low, w_branch, w_rec, x, grad_middle, gain = ins
     _, grad_gain = outs
+    grad_gain[...] = jnp.zeros_like(grad_gain)
 
     def partial(at, n, term):
         rows_product(term, at, n, [(branch_low, w_branch), (rec_low, w_rec)])
 
     def finish(total, near, at, n):
         back, gain_sum = norm_back(total, x[pl.ds(at, n)].astype(F32), gain[...])
-        grad_gain[...] = gain_sum if near == 0 else grad_gain[...] + gain_sum
+        grad_gain[...] = grad_gain[...] + gain_sum
         return (grad_middle[near : near + n] + back).astype(BF16)
 
     return partial, finish
 
 
-TAPS, SHIFT, RBIAS, EBIAS, SOFT = 0, 4, 5, 6, 7
+TAPS, SHIFT, RBIAS, EBIAS, SOFT, SLOPE = 0, 4, 5, 6, 7, 8
 ROWS = 64
 GROUP = 8
 
@@ -474,16 +639,15 @@
     return pltpu.roll(v, n % v.shape[0], 0)
 
 
-def forward_kernel(g, rec, branch, w_rate, w_entry, vecs, mixed, conv, rate, entry, state, edge,
-                   ext, acum, bcum, tot, halo, gath, send, recv):
+def forward_steps(g, wire, rec, branch, w_rate, w_entry, vecs, mixed, conv, rate, entry, state, edge,
+                  ext, acum, bcum, tot, halo, gath):
     L, CH = rec.shape
     q = lax.axis_index("ctx")
-    greet(ctx_peers(g))
-    wire = Wire(send, recv)
     ext[8:] = rec[...]
     if g.Q > 1:
         cp = wire.copy(ext.at[pl.ds(L, 8)], halo, {"ctx": (q + 1) % g.Q})
         cp.start()
+        yield
         cp.wait()
         ext[0:8] = jnp.where(q > 0, halo[...], 0.0)
     else:
@@ -492,7 +656,7 @@
 
     def chunk(i, carry):
         ca, cb = carry
-        r0 = pl.multiple_of(i * ROWS, ROWS)
+        r0 = i * ROWS
         wide = ext[pl.ds(r0, ROWS + 8)]
         c = vecs[SHIFT : SHIFT + 1] + vecs[TAPS : TAPS + 1] * wide[8:]
         for k in range(1, 4):
@@ -523,7 +687,10 @@
             cb = B[GROUP - 1 : GROUP]
         return ca, cb
 
-    ca, cb = lax.fori_loop(0, L // ROWS, chunk, (jnp.ones((1, CH), F32), jnp.zeros((1, CH), F32)))
+    ca, cb = jnp.ones((1, CH), F32), jnp.zeros((1, CH), F32)
+    for i in range(L // ROWS):
+        ca, cb = chunk(i, (ca, cb))
+        yield
     tot[0:1] = ca
     tot[1:2] = cb
     start = jnp.zeros((1, CH), F32)
@@ -533,6 +700,7 @@
             new = gath[d, 0:1] * start + gath[d, 1:2]
             start = jnp.where(d < q, new, start)
     edge[...] = jnp.broadcast_to(start, (8, CH))
+    yield
 
     def fix(i, _):
         r0 = pl.multiple_of(i * ROWS, ROWS)
@@ -542,40 +710,75 @@
         return 0
 
     lax.fori_loop(0, L // ROWS, fix, 0)
-
-
-def forward_call(g, rec, branch, w_rate, w_entry, vecs, cid):
+    yield
+
+
+def forward_scratch(g, L, CH):
+    return [
+        pltpu.VMEM((L + 8, CH), F32),
+        pltpu.VMEM((L, CH), F32),
+        pltpu.VMEM((L, CH), F32),
+        pltpu.VMEM((8, CH), F32),
+        pltpu.VMEM((8, CH), F32),
+        pltpu.VMEM((g.Q, 8, CH), F32),
+    ]
+
+
+def mix_call(g, rec, branch, w_rate, w_entry, vecs, x, gain, out_shard, mlp_shards, cid):
     L, CH = rec.shape
+    width = x.shape[1]
+    chunk = L // 2
+    n = len(mlp_shards)
     wide = jax.ShapeDtypeStruct((L, CH), F32)
-    return pl.pallas_call(
-        functools.partial(forward_kernel, g),
-        out_shape=[jax.ShapeDtypeStruct((L, CH), BF16), wide, wide, wide, wide, jax.ShapeDtypeStruct((8, CH), F32)],
-        in_specs=[VM] * 5,
-        out_specs=[VM] * 6,
-        scratch_shapes=[
-            pltpu.VMEM((L + 8, CH), F32),
-            pltpu.VMEM((L, CH), F32),
-            pltpu.VMEM((L, CH), F32),
-            pltpu.VMEM((8, CH), F32),
-            pltpu.VMEM((8, CH), F32),
-            pltpu.VMEM((g.Q, 8, CH), F32),
-            pltpu.SemaphoreType.DMA((g.Q,)),
-            pltpu.SemaphoreType.DMA((g.Q,)),
-        ],
-        compiler_params=pltpu.CompilerParams(
-            collective_id=cid, has_side_effects=True, vmem_limit_bytes=VMEM_LIMIT
-        ),
-        name="rec_forward",
-    )(rec, branch, w_rate, w_entry, vecs)
-
-
-def backward_kernel(g, mid_low, w_out, branch, rec, conv, rate, entry, state, edge, w_rate, w_entry, vecs,
+    whole = [jax.ShapeDtypeStruct((g.N * s.shape[0], s.shape[1]), s.dtype) for s in [out_shard] + mlp_shards]
+    n_fwd = len(forward_scratch(g, L, CH))
+    count = 2 * g.Q + tp_count(g, L) + (n + 1) * gather_count(g)
+
+    def kernel(rec, branch, w_rate, w_entry, vecs, x, gain, shard, *refs):
+        shards = refs[:n]
+        mixed, conv, rate, entry, state, edge, low_two, middle, w_out = refs[n : n + 9]
+        full = refs[n + 9 : 2 * n + 9]
+        fwd = refs[2 * n + 9 : 2 * n + 9 + n_fwd]
+        term, sendbuf, recvbuf, send, recv, here = refs[2 * n + 9 + n_fwd :]
+        greet(ctx_peers(g) + plane_peers(g) + tp_peers(g))
+        wire = Wire(send, recv)
+        fwd_steps = forward_steps(g, wire, rec, branch, w_rate, w_entry, vecs, mixed, conv, rate, entry, state, edge, *fwd)
+        first = gather_steps(g, wire, here.at[pl.ds(0, 1)], [shard], [w_out])
+        rest = gather_steps(g, wire, here.at[pl.ds(1, n)], shards, full)
+        next(fwd_steps)
+        next(first)
+        for _ in range(L // ROWS + 1):
+            next(fwd_steps)
+        next(first)
+        for _ in range(n):
+            next(rest)
+        run(fwd_steps)
+        run(first)
+        partial, finish = mix_out_body((mixed, w_out, x, gain), (low_two, middle))
+        braid(
+            tp_steps(g, wire, L, low_two, partial, finish, (term, sendbuf, recvbuf)),
+            (rest, MIX_XY),
+        )
+
+    return call(
+        kernel,
+        [rec, branch, w_rate, w_entry, vecs, x, gain, out_shard, *mlp_shards],
+        [jax.ShapeDtypeStruct((L, CH), BF16), wide, wide, wide, wide, jax.ShapeDtypeStruct((8, CH), F32),
+         jax.ShapeDtypeStruct((L, width), BF16), jax.ShapeDtypeStruct((chunk, width), F32), *whole],
+        forward_scratch(g, L, CH) + tp_bufs(g, L, width) + sems(count) + [pltpu.SemaphoreType.DMA((n + 1,))],
+        cid,
+        "mix",
+        [VM] * (n + 8),
+        [VM] * 9 + [ANY] * n,
+    )
+
+
+def backward_steps(g, wire, mid_low, w_out, branch, rec, conv, rate, entry, state, edge, w_rate, w_entry, vecs,
                     branch_low, rec_low, g_rate, g_entry, g_vecs,
-                    sgrad, acum, bcum, gconv, conv_h, conv_l, rb_h, rb_l, eb_h, eb_l, tot, gath, halo, prevx, send, recv):
+                    sgrad, acum, bcum, conv_h, conv_l, rb_h, rb_l, eb_h, eb_l, tot, gath, halo, prevx):
     L, CH = rec.shape
+    gconv = sgrad
     q = lax.axis_index("ctx")
-    greet(ctx_peers(g))
-    wire = Wire(send, recv)
     tail = None
     if g.Q > 1:
         tail = wire.copy(rec.at[pl.ds(L - 8, 8)], prevx, {"ctx": (q + 1) % g.Q})
@@ -583,10 +786,20 @@
     sub = lax.broadcasted_iota(jnp.int32, (GROUP, 1), 0)
     chunks = L // ROWS
 
+    def product_cols(j, _):
+        cols = pl.ds(pl.multiple_of(j * 128, 128), 128)
+        sgrad[:L, cols] = dot(mid_low[...], w_out[:, cols])
+        return 0
+
+    if CH % 128 == 0:
+        lax.fori_loop(0, CH // 128, product_cols, 0)
+    else:
+        sgrad[:L] = dot(mid_low[...], w_out[...])
+
     def chunk(j, carry):
         ua, ub = carry
-        r0 = pl.multiple_of((chunks - 1 - j) * ROWS, ROWS)
-        gm = dot(mid_low[pl.ds(r0, ROWS)], w_out[...])
+        r0 = (chunks - 1 - j) * ROWS
+        gm = sgrad[pl.ds(r0, ROWS)]
         act, slope = gelu_both(branch[pl.ds(r0, ROWS)])
         branch_low[pl.ds(r0, ROWS)] = (gm * state[pl.ds(r0, ROWS)] * slope).astype(BF16)
         sg = gm * act
@@ -610,7 +823,11 @@
             ub = B[0:1]
         return ua, ub
 
-    ua, ub = lax.fori_loop(0, chunks, chunk, (jnp.ones((1, CH), F32), jnp.zeros((1, CH), F32)))
+    yield
+    ua, ub = jnp.ones((1, CH), F32), jnp.zeros((1, CH), F32)
+    for i in range(chunks):
+        ua, ub = chunk(i, (ua, ub))
+        yield
     tot[0:1] = ua
     tot[1:2] = ub
     arriving = jnp.zeros((1, CH), F32)
@@ -630,7 +847,7 @@
 
     def back(i, carry):
         gdec, gbr, gbe, gshift, gt0, gt1, gt2, gt3, last_state, last_rec = carry
-        r0 = pl.multiple_of(i * ROWS, ROWS)
+        r0 = i * ROWS
         aw = row_shift(acum[pl.ds(r0, ROWS + 8)], -1)[:ROWS]
         bw = row_shift(bcum[pl.ds(r0, ROWS + 8)], -1)[:ROWS]
         car = sgrad[pl.ds(r0, ROWS)] + bw + aw * arriving
@@ -673,19 +890,36 @@
             gts[k] = gts[k] + jnp.sum(gc * xk, axis=0, keepdims=True)
         return (gdec, gbr, gbe, gshift, *gts, st[ROWS - 8 :], x[ROWS - 8 :])
 
-    carry = lax.fori_loop(0, chunks, back, (zero,) * 8 + (edge[...], prev_rows))
+    yield
+    carry = (zero,) * 8 + (edge[...], prev_rows)
+    for i in range(chunks):
+        carry = back(i, carry)
+        yield
     gdec, gbr, gbe, gshift, gt0, gt1, gt2, gt3 = carry[:8]
     if g.Q > 1:
         cp = wire.copy(gconv.at[pl.ds(0, 8)], halo, {"ctx": (q + g.Q - 1) % g.Q})
         cp.start()
+    gdec = gdec * vecs[SLOPE : SLOPE + 1]
     for k, v in enumerate((gt0, gt1, gt2, gt3, gshift, gbr, gbe, gdec)):
         g_vecs[k : k + 1] = v
+    yield
 
     def product(h, l):
         return dot_tokens(conv_h[...], h[...]) + dot_tokens(conv_l[...], h[...]) + dot_tokens(conv_h[...], l[...])
 
-    g_rate[...] = product(rb_h, rb_l)
-    g_entry[...] = product(eb_h, eb_l)
+    bw = g_rate.shape[0]
+    head = lax.broadcasted_iota(jnp.int32, (bw, CH), 1) // bw
+
+    def diagonal(dense):
+        total = jnp.zeros((bw, CH), F32)
+        for h in range(CH // bw):
+            total = total + jnp.where(head == h, dense[h * bw : (h + 1) * bw], 0.0)
+        return total
+
+    g_rate[...] = diagonal(product(rb_h, rb_l))
+    yield
+    g_entry[...] = diagonal(product(eb_h, eb_l))
+    yield
     if g.Q > 1:
         cp.wait()
         gconv[L:] = jnp.where(q < g.Q - 1, halo[...], 0.0)
@@ -702,19 +936,64 @@
         return 0
 
     lax.fori_loop(0, chunks, last, 0)
-
-
-def backward_call(g, mid_low, w_out, branch, rec, conv, rate, entry, state, edge, w_rate, w_entry, vecs, cid):
+    yield
+
+
+def back_call(g, mid_low, w_out, branch, rec, conv, rate, entry, state, edge, w_rate, w_entry, vecs, bw, middle,
+              cot, live, hidden, w_down, mixed, cid):
     L, CH = rec.shape
+    half, width = middle.shape
     low = jax.ShapeDtypeStruct((L, CH), BF16)
-    dense = jax.ShapeDtypeStruct((CH, CH), F32)
-    return pl.pallas_call(
-        functools.partial(backward_kernel, g),
-        out_shape=[low, low, dense, dense, jax.ShapeDtypeStruct((8, CH), F32)],
-        in_specs=[VM] * 12,
-        out_specs=[VM] * 5,
-        scratch_shapes=[
-            pltpu.VMEM((L, CH), F32),
+    diag = jax.ShapeDtypeStruct((bw, CH), F32)
+    F = hidden.shape[1]
+    rows = width // g.N
+    count = g.Q + 2 + tp_count(g, L) + 2 * reduce_count(g)
+    operands = [mid_low, w_out, branch, rec, conv, rate, entry, state, edge, w_rate, w_entry, vecs,
+                middle, cot, live, hidden, w_down, mixed]
+
+    def kernel(*refs):
+        ins, (middle, cot, live, hidden, w_down, mixed) = refs[:12], refs[12:18]
+        outs, (output, g_down, g_out) = refs[18:23], refs[23:26]
+        bufs = refs[26:39]
+        cot_t, term, sendbuf, recvbuf, *more = refs[39:]
+        mid_t = cot_t
+        send, recv = more[-2:]
+        greet(ctx_peers(g) + tp_peers(g) + plane_peers(g))
+        wire = Wire(send, recv)
+
+        def z():
+            yield
+            body = mlp_out_body((hidden.ref(), w_down.ref(), middle, live), (output,))
+            yield from tp_steps(g, wire, L, output, *body, (term, sendbuf, recvbuf))
+
+        def down():
+            yield from turn_steps(rows, cot_t, cot, live)
+            hidden.ref()
+            yield from reduce_steps(g, wire, [(product_term(cot.dst, cot_t, hidden.dst, rows, live), g_down, more[0:3])])
+
+        down_steps = down()
+        if needs_turn(rows):
+            for _ in range(len(range(0, width, 512)) + g.C * g.A * g.B):
+                next(down_steps)
+
+        def out():
+            yield from turn_steps(rows, mid_t, ins[0])
+            mixed.ref()
+            yield from reduce_steps(g, wire, [(product_term(ins[0], mid_t, mixed.dst, rows), g_out, more[3:6])])
+
+        braid(
+            chain(backward_steps(g, wire, *ins, *outs, *bufs), iter(range(4))),
+            (z(), BACK_Z),
+            (down_steps, BACK_DOWN),
+            (out(), BACK_OUT),
+        )
+
+    return call(
+        kernel,
+        operands,
+        [low, low, diag, diag, jax.ShapeDtypeStruct((8, CH), F32), jax.ShapeDtypeStruct((L, width), BF16),
+         jax.ShapeDtypeStruct((rows, F), F32), jax.ShapeDtypeStruct((rows, CH), F32)],
+        [
             pltpu.VMEM((L + 8, CH), F32),
             pltpu.VMEM((L + 8, CH), F32),
             pltpu.VMEM((L + 8, CH), F32),
@@ -725,14 +1004,16 @@
             pltpu.VMEM((g.Q, 8, CH), F32),
             pltpu.VMEM((8, CH), F32),
             pltpu.VMEM((8, CH), F32),
-            pltpu.SemaphoreType.DMA((g.Q + 1,)),
-            pltpu.SemaphoreType.DMA((g.Q + 1,)),
-        ],
-        compiler_params=pltpu.CompilerParams(
-            collective_id=cid, has_side_effects=True, vmem_limit_bytes=VMEM_LIMIT
-        ),
-        name="rec_backward",
-    )(mid_low, w_out, branch, rec, conv, rate, entry, state, edge, w_rate, w_entry, vecs)
+        ]
+        + turn_scratch(rows, width, L)
+        + tp_bufs(g, L, width)
+        + reduce_bufs(g, rows, F)
+        + reduce_bufs(g, rows, CH)
+        + sems(count),
+        cid,
+        "rec_backward",
+        later=(15, 16, 13, 17),
+    )
 
 
 def reduce_count(g):
@@ -768,28 +1049,7 @@
         return g.block((a + g.A - k // g.B) % g.A, (b + g.B - k % g.B) % g.B, core)
 
     def each_tile(width, fn):
-        tile = tile_of(width)
-        lax.fori_loop(0, width // tile, lambda j, _: fn(pl.ds(pl.multiple_of(j * tile, tile), tile)) or 0, 0)
-
-    bases = []
-    for term, out, (to_sib, sums, land) in items:
-        base = wire.used
-        bases.append(base)
-        if g.C == 2:
-            wire.used += nb
-
-            def one(i, _):
-                k = (i + 1) % nb
-
-                def tile(cols):
-                    to_sib[k, :, cols] = term(owner(k, 1 - c), cols).astype(BF16)
-
-                each_tile(out.shape[1], tile)
-                wire.at(base + k, to_sib.at[k], sums.at[k], g.dev(a, b, 1 - c)).start()
-                return 0
-
-            lax.fori_loop(0, nb, one, 0)
-        yield
+        fn(slice(None))
 
     rings = [(g.A, g.B), (g.B, g.A)]
     devs = [
@@ -800,47 +1060,46 @@
     def slot(h, df, dg):
         return df * g.B + dg if h == 0 else dg * g.B + df
 
+    bases = []
     state = []
-    for (term, out, (to_sib, sums, land)), base in zip(items, bases):
+    for term, out, (to_sib, sums, land) in items:
         half = out.shape[0] // 2
-
-        def got(k):
+        base = wire.used
+        bases.append(base)
+        if g.C == 2:
+            wire.used += nb
+            for k in [(i + 1) % nb for i in range(nb)]:
+
+                def tile(cols):
+                    to_sib[k, :, cols] = term(owner(k, 1 - c), cols).astype(BF16)
+
+                each_tile(out.shape[1], tile)
+                wire.at(base + k, to_sib.at[k], sums.at[k], g.dev(a, b, 1 - c)).start()
+                yield
+        used = 0
+        first = ({}, {})
+        for k in [(i + 1) % nb for i in range(nb)]:
             if g.C == 2:
                 wire.at(base + k, to_sib.at[k], sums.at[k], g.dev(a, b, 1 - c)).wait_recv()
-
-        def one(k, _):
-            got(k)
 
             def tile(cols):
                 s = term(owner(k, c), cols)
                 if g.C == 2:
                     s = s + sums[k, :, cols].astype(F32)
-                sums[k, :, cols] = s.astype(BF16)
+                if k == 0:
+                    out[:, cols] = s
+                else:
+                    sums[k, :, cols] = s.astype(BF16)
 
             each_tile(out.shape[1], tile)
-            return 0
-
-        lax.fori_loop(1, nb, one, 0)
-        used = 0
-        first = ({}, {})
-        for h in (0, 1):
-            nf, ng = rings[h]
-            if nf > 1:
-                for dg in [d % ng for d in range(1, ng + 1)]:
-                    k = slot(h, 1, dg)
+            for h in (0, 1):
+                nf, ng = rings[h]
+                df, dg = (k // g.B, k % g.B) if h == 0 else (k % g.B, k // g.B)
+                if nf > 1 and df == 1:
                     first[h][dg] = (start(sums.at[k, pl.ds(h * half, half)], land.at[used], devs[h][0]), used)
                     used += 1
-        got(0)
-
-        def tile(cols):
-            s = term(owner(0, c), cols)
-            if g.C == 2:
-                s = s + sums[0, :, cols].astype(F32)
-            out[:, cols] = s
-
-        each_tile(out.shape[1], tile)
+            yield
         state.append([first, used])
-        yield
 
     def add(out, sums, k, h, half, arrived):
         at = slice(h * half, (h + 1) * half)
@@ -896,63 +1155,212 @@
                 wire.at(base + k, to_sib.at[k], sums.at[k], g.dev(a, b, 1 - c)).wait_send()
 
 
-def reduce_call(g, pairs, given, cid, name):
-    ops, where, items = [], [], []
-
-    def place(x):
-        for k, o in enumerate(ops):
-            if o is x:
-                return k
-        ops.append(x)
-        return len(ops) - 1
-
-    for l, r in pairs:
-        where.append((place(l), place(r)))
-        items.append((l.shape[0] // g.N, r.shape[1]))
-    for v in given:
-        where.append((place(v), None))
-        items.append((v.shape[0] // g.N, v.shape[1]))
-    n_in, n_out = len(ops), len(items)
-    count = n_out * reduce_count(g)
+def needs_turn(rows):
+    return rows % 128 != 0
+
+
+def turn_scratch(rows, width, L):
+    return [pltpu.VMEM((width, L) if needs_turn(rows) else (16, 128), BF16)]
+
+
+def product_term(left, turned, right, rows, mask=None):
+    def term(block, cols):
+        at = pl.ds(pl.multiple_of(block * rows, rows), rows)
+        if needs_turn(rows):
+            return dot(turned[at], right[:, cols])
+        v = left[:, at]
+        if mask is not None:
+            v = (v.astype(F32) * mask[...]).astype(BF16)
+        return dot_tokens(v, right[:, cols])
+
+    return term
+
+
+def turn_steps(rows, turned, left, mask=None):
+    if isinstance(left, Later):
+        left = left.ref()
+    if needs_turn(rows):
+        yield from transpose_steps(turned, left, mask)
+
+
+def given_term(part, rows):
+    def term(block, cols):
+        return part[pl.ds(pl.multiple_of(block * rows, rows), rows), cols]
+
+    return term
+
+
+def mlp_back_call(g, low_two, gate_low, up_low, w_gate, w_up, middle, cot, live, gain, cid):
+    L, width = low_two.shape
+    F = gate_low.shape[1]
+    half = L // 2
+    rows = width // g.N
+    count = tp_count(g, L) + 2 * reduce_count(g)
+    grad = jax.ShapeDtypeStruct((rows, F), F32)
+
+    def kernel(low_two, gate_low, up_low, w_gate, w_up, middle, cot, live, gain,
+               mid_low, grad_middle, grad_gain, g_gate, g_up,
+               two_t, term, sendbuf, recvbuf, *refs):
+        send, recv = refs[-2:]
+        bufs = refs[:-2]
+        greet(plane_peers(g) + tp_peers(g))
+        wire = Wire(send, recv)
+        middle, cot = middle.ref(), cot.ref()
+        back = mlp_back_body((gate_low, up_low, w_gate, w_up, middle, cot, live, gain), (mid_low, grad_middle, grad_gain))
+
+        def gate():
+            yield from turn_steps(rows, two_t, low_two)
+            yield from reduce_steps(g, wire, [(product_term(low_two.dst, two_t, gate_low, rows), g_gate, bufs[0:3])])
+
+        def up():
+            yield from reduce_steps(g, wire, [(product_term(low_two.dst, two_t, up_low, rows), g_up, bufs[3:6])])
+
+        braid(
+            tp_steps(g, wire, L, mid_low, *back, (term, sendbuf, recvbuf)),
+            (gate(), MLP_GATE),
+            (up(), MLP_UP),
+        )
+
+    scratch = turn_scratch(rows, width, L) + tp_bufs(g, L, width)
+    for _ in range(2):
+        scratch += reduce_bufs(g, rows, F)
+    return call(
+        kernel,
+        [low_two, gate_low, up_low, w_gate, w_up, middle, cot, live, gain],
+        [jax.ShapeDtypeStruct((L, width), BF16), jax.ShapeDtypeStruct((half, width), F32),
+         jax.ShapeDtypeStruct((1, width), F32), grad, grad],
+        scratch + sems(count),
+        cid,
+        "mlp_back",
+        later=(0, 5, 6),
+    )
+
+
+def plane_others(g):
+    s, q = lax.axis_index("shard"), lax.axis_index("ctx")
+    me = s * g.Q + q
+    out = []
+    for k in range(1, g.N):
+        d = (me + k) % g.N
+        out.append({"shard": d // g.Q, "ctx": d % g.Q})
+    return me, out
+
+
+def total_steps(g, wire, mine, land_t, land_p, out):
+    t = lax.axis_index("tp")
+    me, others = plane_others(g)
+    land_t[t] = mine[...]
+    cps = [wire.copy(mine, land_t.at[t], {"tp": (t + k) % g.T}) for k in range(1, g.T)]
+    for cp in cps:
+        cp.start()
+    yield
+    for cp in cps:
+        cp.wait()
+    total = land_t[0]
+    for d in range(1, g.T):
+        total = total + land_t[d]
+    mine[...] = total
+    land_p[me] = total
+    cps = [wire.copy(mine, land_p.at[me], d) for d in others]
+    for cp in cps:
+        cp.start()
+    yield
+    for cp in cps:
+        cp.wait()
+    total = land_p[0]
+    for d in range(1, g.N):
+        total = total + land_p[d]
+    out[...] = total
+
+
+def rec_back_call(g, branch_low, rec_low, w_branch, w_rec, x, grad_middle, gain, part_two, low_one, small, cid):
+    L, width = x.shape
+    CH = branch_low.shape[1]
+    rows = width // g.N
+    srows = small.shape[0] // g.N
+    shapes = [(rows, CH), (rows, CH), (srows, small.shape[1])]
+    count = tp_count(g, L) + len(shapes) * reduce_count(g) + g.T + g.N
+
+    def kernel(branch_low, rec_low, w_branch, w_rec, x, grad_middle, gain, part_two, low_one, small,
+               input_grad, gains, g_branch, g_rec, g_small,
+               part_one, one_t, both, land_t, land_p, term, sendbuf, recvbuf, *refs):
+        send, recv = refs[-2:]
+        bufs = refs[:-2]
+        t = lax.axis_index("tp")
+        greet(plane_others(g)[1] + [{"tp": (t + k) % g.T} for k in range(1, g.T)])
+        wire = Wire(send, recv)
+        x, grad_middle = x.ref(), grad_middle.ref()
+        back = rec_back_body((branch_low, rec_low, w_branch, w_rec, x, grad_middle, gain), (input_grad, part_one))
+
+        def one(term, out, bufs):
+            yield from reduce_steps(g, wire, [(term, out, bufs)])
+
+        def branch():
+            yield from turn_steps(rows, one_t, low_one)
+            yield from one(product_term(low_one.dst, one_t, branch_low, rows), g_branch, bufs[0:3])
+
+        def main():
+            steps = tp_steps(g, wire, L, input_grad, *back, (term, sendbuf, recvbuf))
+            for _ in range(L // 2 // PIECE + END["take_far"]):
+                next(steps)
+                yield
+            both[:, :width] = part_one[...]
+            both[:, width:] = part_two[...]
+            totals = total_steps(g, wire, both, land_t, land_p, gains)
+            next(totals)
+            for _ in steps:
+                next(totals, None)
+                yield
+            run(totals)
+
+        braid(
+            main(),
+            (branch(), REC_BRANCH),
+            (one(product_term(low_one.dst, one_t, rec_low, rows), g_rec, bufs[3:6]), REC_REC),
+            (one(given_term(small, srows), g_small, bufs[6:9]), REC_SMALL),
+        )
+
+    scratch = [pltpu.VMEM((1, width), F32)] + turn_scratch(rows, width, L)
+    scratch += [pltpu.VMEM((1, 2 * width), F32), pltpu.VMEM((g.T, 1, 2 * width), F32), pltpu.VMEM((g.N, 1, 2 * width), F32)]
+    scratch += tp_bufs(g, L, width)
+    for s in shapes:
+        scratch += reduce_bufs(g, *s)
+    return call(
+        kernel,
+        [branch_low, rec_low, w_branch, w_rec, x, grad_middle, gain, part_two, low_one, small],
+        [jax.ShapeDtypeStruct((L, width), BF16), jax.ShapeDtypeStruct((1, 2 * width), F32)]
+        + [jax.ShapeDtypeStruct(s, F32) for s in shapes],
+        scratch + sems(count),
+        cid,
+        "rec_back",
+        later=(8, 4, 5),
+    )
+
+
+def settle(arrays):
+    n = len(arrays)
 
     def kernel(*refs):
-        ins, outs = refs[:n_in], refs[n_in : n_in + n_out]
-        bufs = refs[n_in + n_out : n_in + 4 * n_out]
-        send, recv = refs[n_in + 4 * n_out :]
-        greet(plane_peers(g))
-
-        def term_of(where, rows):
-            l, r = where
-
-            def term(block, cols):
-                at = pl.ds(pl.multiple_of(block * rows, rows), rows)
-                if r is None:
-                    return ins[l][at, cols]
-                return dot(ins[l][at], ins[r][:, cols])
-
-            return term
-
-        work = [
-            (term_of(where[k], items[k][0]), outs[k], bufs[3 * k : 3 * k + 3]) for k in range(n_out)
-        ]
-        for _ in reduce_steps(g, Wire(send, recv), work):
-            pass
-
-    scratch = []
-    for rows, width in items:
-        scratch += reduce_bufs(g, rows, width)
+        ins, outs, kept, sem = refs[:n], refs[n : 2 * n], refs[2 * n : 3 * n], refs[3 * n]
+        cps = [pltpu.make_async_copy(ins[k], kept[k], sem.at[k]) for k in range(n)]
+        back = [pltpu.make_async_copy(kept[k], outs[k], sem.at[n + k]) for k in range(n)]
+        for cp in cps:
+            cp.start()
+        for k in range(n):
+            cps[k].wait()
+            back[k].start()
+        for cp in back:
+            cp.wait()
+
     return pl.pallas_call(
         kernel,
-        out_shape=[jax.ShapeDtypeStruct(s, F32) for s in items],
-        in_specs=[VM] * n_in,
-        out_specs=[VM] * n_out,
-        scratch_shapes=scratch
-        + [pltpu.SemaphoreType.DMA((count,)), pltpu.SemaphoreType.DMA((count,))],
-        compiler_params=pltpu.CompilerParams(
-            collective_id=cid, has_side_effects=True, vmem_limit_bytes=VMEM_LIMIT
-        ),
-        name=name,
-    )(*ops)
+        out_shape=[jax.ShapeDtypeStruct(v.shape, v.dtype) for v in arrays],
+        in_specs=[ANY] * n,
+        out_specs=[ANY] * n,
+        scratch_shapes=[pltpu.VMEM(v.shape, v.dtype) for v in arrays] + [pltpu.SemaphoreType.DMA((2 * n,))],
+        compiler_params=pltpu.CompilerParams(vmem_limit_bytes=VMEM_LIMIT),
+        name="settle",
+    )(*arrays)
 
 
 def up_to(n, k):
@@ -976,7 +1384,6 @@
     slots, block_len, width = inputs.shape
     L = slots * block_len
     N, T = g.N, g.T
-    chunk = L // T
     heads, rb, bw = rgate_weight.shape
     ch = heads * bw
     taps = conv_weight.shape[0]
@@ -985,8 +1392,7 @@
     srows = up_to(-(-sum(sizes) // 256), 32)
     pack = small_pack(small, srows, 256)
 
-    got = gather_call(g, [pack, branch_weight, rec_in_weight, out_weight, mlp_gate_weight, mlp_up_weight, mlp_down_weight], 0)
-    packs, w_branch, w_rec, w_out, w_gate, w_up, w_down = got
+    packs, w_branch, w_rec = gather_call(g, [pack, branch_weight, rec_in_weight], 0)
     packs = packs.reshape(N, -1)
     cut, at = [], 0
     for p, s in zip(small, sizes):
@@ -1001,7 +1407,8 @@
 
     decay_f = channels(cut[6])
     vecs = jnp.concatenate(
-        [taps_f, channels(cut[3]), channels(cut[4]), channels(cut[5]), jax.nn.softplus(-decay_f)], axis=0
+        [taps_f, channels(cut[3]), channels(cut[4]), channels(cut[5]), jax.nn.softplus(-decay_f), jax.nn.sigmoid(-decay_f),
+         jnp.zeros((7, ch), F32)], axis=0
     )
     gain_one = cut[7].reshape(1, width).astype(F32)
     gain_two = cut[8].reshape(1, width).astype(F32)
@@ -1010,65 +1417,53 @@
     cot = cotangent.reshape(L, width)
     positions = lax.axis_index("ctx") * block_len + jnp.arange(block_len, dtype=jnp.int32)
     live = (positions[None, :] < lengths[:, None]).astype(F32).reshape(L, 1)
-    t = lax.axis_index("tp")
     x_f = x_low.astype(F32)
     low_one = (x_f * lax.rsqrt(mean_square(x_f) + EPS) * gain_one).astype(BF16)
     branch_pre = dot(low_one, w_branch)
     rec_pre = dot(low_one, w_rec)
-    mixed, conv, rate, entry, state, edge = forward_call(g, rec_pre, branch_pre, w_rate, w_entry, vecs, 1)
-
-    low = jax.ShapeDtypeStruct((L, width), BF16)
-    mid = jax.ShapeDtypeStruct((chunk, width), F32)
-    vec = jax.ShapeDtypeStruct((1, width), F32)
-    low_two, middle = tp_call(g, mix_out_body, (mixed, w_out, x_low, gain_two), [low, mid], chunk, width, 2, "mix_out")
+    mixed, conv, rate, entry, state, edge, low_two, middle, w_out, w_gate, w_up, w_down = mix_call(
+        g, rec_pre, branch_pre, w_rate, w_entry, vecs, x_low, gain_two, out_weight,
+        [mlp_gate_weight, mlp_up_weight, mlp_down_weight], 1
+    )
     gate_pre = dot(low_two, w_gate)
     up_pre = dot(low_two, w_up)
     act, slope = gelu_both(gate_pre)
     hidden = (act * up_pre).astype(BF16)
-    (output,) = tp_call(g, mlp_out_body, (hidden, w_down, middle, live), [low], chunk, width, 3, "mlp_out")
     grad_low = (cot.astype(F32) * live).astype(BF16)
     grad_hidden = dot(grad_low, w_down)
     gate_low = (grad_hidden * up_pre * slope).astype(BF16)
     up_low = (grad_hidden * act).astype(BF16)
-    mid_low, grad_middle, part_two = tp_call(
-        g, mlp_back_body, (gate_low, up_low, w_gate, w_up, middle, cot, live, gain_two), [low, mid, vec], chunk, width, 4, "mlp_back"
+    mid_low, grad_middle, part_two, g_gate, g_up = mlp_back_call(
+        g, low_two, gate_low, up_low, w_gate, w_up, middle, cot, live, gain_two, 2
     )
-    g_gate, g_up, g_down = reduce_call(
-        g, [(low_two.T, gate_low), (low_two.T, up_low), (grad_low.T, hidden)], [], 5, "reduce_mlp"
+    branch_low, rec_low, d_rate, d_entry, d_vecs, output, g_down, g_out = back_call(
+        g, mid_low, w_out, branch_pre, rec_pre, conv, rate, entry, state, edge, w_rate, w_entry, vecs, bw, middle,
+        cot, live, hidden, w_down, mixed, 3
     )
-    branch_low, rec_low, d_rate, d_entry, d_vecs = backward_call(
-        g, mid_low, w_out, branch_pre, rec_pre, conv, rate, entry, state, edge, w_rate, w_entry, vecs, 6
+
+    d_vecs = d_vecs.reshape(8, heads, N, rb).transpose(2, 0, 1, 3).reshape(N, -1)
+    d_vecs = jnp.pad(d_vecs, ((0, 0), (0, up_to(d_vecs.shape[1], ch) - d_vecs.shape[1]))).reshape(N, -1, ch)
+    flat = jnp.concatenate([d_rate.reshape(N, rb, ch), d_entry.reshape(N, rb, ch), d_vecs], axis=1)
+    used = flat.shape[1]
+    flat = jnp.pad(flat, ((0, 0), (0, up_to(used, 32) - used), (0, 0))).reshape(-1, ch)
+    input_grad, gains, g_branch, g_rec, g_small = rec_back_call(
+        g, branch_low, rec_low, w_branch, w_rec, x_low, grad_middle, gain_one, part_two, low_one, flat, 4
     )
-    input_grad, part_one = tp_call(
-        g, rec_back_body, (branch_low, rec_low, w_branch, w_rec, x_low, grad_middle, gain_one), [low, vec], chunk, width, 7, "rec_back"
-    )
-
-    eye = jnp.eye(heads, dtype=F32)[:, None, :, None]
-
-    def diagonal(d):
-        return jnp.sum(d.reshape(heads, bw, heads, bw) * eye, axis=0).reshape(N, rb * ch)
-
-    d_gates = jnp.concatenate([diagonal(d_rate), diagonal(d_entry)], axis=1)
-    d_vecs = d_vecs.at[7].multiply(jax.nn.sigmoid(-decay_f[0]))
-    d_rows = d_vecs.reshape(8, heads, N, rb).transpose(2, 0, 1, 3).reshape(N, -1)
-    gains = lax.psum(jnp.concatenate([part_one, part_two], axis=0), "tp").reshape(2, N, -1).transpose(1, 0, 2).reshape(N, -1)
-    flat = jnp.concatenate([d_gates, d_rows, gains], axis=1)
-    prows = up_to(-(-flat.shape[1] // 256), 32)
-    flat = jnp.pad(flat, ((0, 0), (0, prows * 256 - flat.shape[1]))).reshape(N * prows, 256)
-    g_branch, g_rec, g_out, g_small = reduce_call(
-        g, [(low_one.T, branch_low), (low_one.T, rec_low), (mid_low.T, mixed)], [flat], 8, "reduce_rec"
-    )
+    gains = lax.dynamic_slice(
+        gains.reshape(2, N, -1), (0, lax.axis_index("shard") * g.Q + lax.axis_index("ctx"), 0), (2, 1, width // N)
+    )[:, 0]
     g_small = g_small.reshape(-1)
     n = rb * ch
     g_rate = g_small[:n].reshape(rb, heads, bw).transpose(1, 0, 2)
     g_entry = g_small[n : 2 * n].reshape(rb, heads, bw).transpose(1, 0, 2)
     rest = g_small[2 * n : 2 * n + 8 * heads * rb].reshape(8, heads, rb)
-    tail = g_small[2 * n + 8 * heads * rb :]
-    m = width // N
     shape = (slots, block_len, width)
+    output, input_grad, g_branch, g_rec, g_out, g_gate, g_up, g_down = settle(
+        [output, input_grad, g_branch, g_rec, g_out, g_gate, g_up, g_down]
+    )
     return (
-        output.reshape(shape), input_grad.reshape(shape), tail[:m], g_branch, g_rec, rest[:taps], rest[4],
-        g_rate, rest[5], g_entry, rest[6], rest[7], g_out, tail[m : 2 * m], g_gate, g_up, g_down,
+        output.reshape(shape), input_grad.reshape(shape), gains[0], g_branch, g_rec, rest[:taps], rest[4],
+        g_rate, rest[5], g_entry, rest[6], rest[7], g_out, gains[1], g_gate, g_up, g_down,
     )
 
 

time: 785 us -> 468 us (0.60)
  Pallas kernels: 637 us -> 394 us
  local copies, waits for them, and re-layouts: 64.1 us -> 29.7 us
  blocking collectives: 16.1 us -> 0 us
  matrix products: 38.4 us -> 27.1 us
  other arithmetic: 17.8 us -> 6.99 us
    pallas_call x8 -> x5, Pallas kernels: 517 us -> 363 us  [the longest x4 354 us: call(): pl.pallas_call(body, out_shape=out_shape, in_specs=in_specs, out_specs=ou...]
    pallas_call x1, Pallas kernels: 119 us -> 31.8 us  [gather_call(): pl.pallas_call(functools.partial(gather_kernel, g, n), out_shape=[jax.Sha...]
    unnamed x53 -> x27, local copies, waits for them, and re-layouts: 21 us -> 4.66 us
    psum x1 -> x0, blocking collectives: 16.1 us -> none  [local(): lax.psum(jnp.concatenate([part_one, part_two], axis=0), 'tp')]
    dot_general x5, matrix products: 38.4 us -> 27.1 us  [dot(): return jnp.dot(a, b, preferred_element_type=F32)]
    reshape x5 -> x4, local copies, waits for them, and re-layouts: 12 us -> 2.28 us  [the longest x1 1.05 us: local(): d_rate.reshape(N, rb, ch)]
where the time goes in v2:
time: 468 us; the launch traced here: 460 us
  Pallas kernels  394 us (84%)
  local copies, waits for them, and re-layouts  29.7 us (6%)
  matrix products  27.1 us (6%)
  other arithmetic  6.99 us (1%)
    pallas_call x4, Pallas kernels, call(): pl.pallas_call(body, out_shape=out_shape, in_specs=in_specs, out_specs=ou...  354 us
    pallas_call x1, Pallas kernels, gather_call(): pl.pallas_call(functools.partial(gather_kernel, g, n), out_shape=[jax.Sha...  31.8 us
    dot_general x5, matrix products, dot(): return jnp.dot(a, b, preferred_element_type=F32)  27.1 us

profile of v2, /device:TPU:0, one launch (start us, length us, event | category | flops | bytes accessed | tf_op | source)
XLA Modules:
  0.0 460.4 jit_solution(18110832250959099334)
XLA Ops:
  0.7 0.8 copy.42
  1.6 0.8 copy.43
  2.5 0.8 reshape.345
  3.3 0.8 reshape.346
  4.0 0.8 reshape.347
  4.8 0.8 reshape.348
  5.5 0.8 reshape.349
  6.3 1.4 concatenate.9
  8.4 31.8 %gather.1 = (bf16[1024,256]{1,0:T(8,128)(2,1)}, bf16[2048,640]{1,0:T(8,128)(2,1)}, bf16[2048,640]{1,0:T(8,128)(2,1)}) custom-call(bf16[128,256]{1,0:T(8,128)(2,1)} %reshape.350.refs_0_, bf16[256,640]{1,0:T(8,128)(2,1)} %refs_1_.1, bf16[256,640]{1,0:T(8,128)(2,1)} %refs_2_.1), custom_call_target="tpu_custom_call" | custom-call | tf_op jit(solution)/shard_map/gather/pallas_call | solution.py:324
  40.2 1.3 reshape.351
  43.0 1.3 concatenate.10.refs_4_.refs_11_
  45.7 2.4 broadcast_multiply_fusion
  48.1 2.9 mul.137.refs_2_.refs_9_
  51.1 1.6 mul.141.refs_3_.refs_10_
  54.4 1.7 copy-done.4
  56.1 2.9 fusion.22.refs_1_.refs_2_
  59.0 2.9 fusion.21.refs_0_.refs_3_
  62.5 108.3 %mix.1 = (bf16[512,640]{1,0:T(8,128)(2,1)}, f32[512,640]{1,0:T(8,128)}, f32[512,640]{1,0:T(8,128)}, f32[512,640]{1,0:T(8,128)}, f32[512,640]{1,0:T(8,128)}, /*in...) custom-call(f32[512,640]{1,0:T(8,128)} %fusion.21.refs_0_.refs_3_, ...), custom_call_target="tpu_custom_call" | custom-call | tf_op jit(solution)/shard_map/mix/pallas_call | solution.py:205
  170.9 8.6 %fusion.23 = f32[512,1536]{1,0:T(8,128)} fusion(bf16[512,2048]{1,0:T(8,128)(2,1)} %get-tuple-element.61.refs_0_, bf16[2048,1536]{1,0:T(8,128)(2,1)} %get-tuple-element.64.refs_3_), kind=kOutput, calls=%fused_computation.63 | convolution fusion | flops 3221225472 | bytes 11534336 | tf_op jit(solution)/shard_map/dot_general | solution.py:21
  180.2 6.0 %fusion.11 = f32[512,1536]{1,0:T(8,128)S(1)} fusion(bf16[2048,1536]{1,0:T(8,128)(2,1)} %get-tuple-element.62.refs_16_, f32[512]{0:T(512)S(1)} %fusion.16, bf16[1,512,2048]{2,1,0:T(8,128)(2,1)S(1)} %copy-done.1), kind=kOutput, calls=%fused_computation.19 | convolution fusion | flops 3224371200 | bytes 11536384 | tf_op jit(solution)/shard_map/dot_general | solution.py:21
  186.3 6.8 %multiply_convert_fusion.1 = (bf16[512,1536]{1,0:T(8,128)(2,1)}, bf16[512,1536]{1,0:T(8,128)(2,1)}, bf16[512,1536]{1,0:T(8,128)(2,1)}) fusion(f32[512,1536]{1,0:T(8,128)S(1)} %copy-done.10, f32[512,1536]{1,0:T(8,128)S(1)} %fusion.11, bf16[512,2048]{1,0:T(8,128)(2,1)S(1)} %copy-done.6, bf16[2048,1536]{1,0:T(8,128)(2,1)S(1)} %copy-done.3), kind=kOutput, calls=%fused_computation.15 | convolution fusion | flops 3240886272 | bytes 19398656 | tf_op jit(solution)/shard_map/dot_general | solution.py:21
  193.1 0.7 fusion.13.refs_7_.refs_14_
  193.8 81.3 %mlp_back.1 = (bf16[512,2048]{1,0:T(8,128)(2,1)}, f32[256,2048]{1,0:T(8,128)}, f32[1,2048]{1,0:T(1,128)}, f32[256,1536]{1,0:T(8,128)}, f32[256,1536]{1,0:T(8,128)}) custom-call(bf16[512,2048]{1,0:T(8,128)(2,1)} %get-tuple-element.61.refs_0_, bf16[512,1536]{1,0:T(8,128)(2,1)} %get-tuple-element.104.refs_1_, bf16[512,1536]{1,0:T(8,128)(2,1)} %get-tuple-element.105.refs_2_, ...), custom_call_target="tpu_custom_call" | custom-call | tf_op jit(solution)/shard_map/mlp_back/pallas_call | solution.py:205
  275.1 88.9 %rec_backward.1 = (bf16[512,640]{1,0:T(8,128)(2,1)}, bf16[512,640]{1,0:T(8,128)(2,1)}, f32[160,640]{1,0:T(8,128)}, f32[160,640]{1,0:T(8,128)}, f32[8,640]{1,0:T(...) custom-call(bf16[512,2048]{1,0:T(8,128)(2,1)} %get-tuple-element.66.refs_0_, ...), custom_call_target="tpu_custom_call" | custom-call | tf_op jit(solution)/shard_map/rec_backward/pallas_call | solution.py:205
  364.1 1.0 reshape.355
  365.1 1.0 reshape.356
  366.2 0.9 reshape.357
  367.3 1.2 select_maximum_fusion
  369.1 75.8 %rec_back.1 = (bf16[512,2048]{1,0:T(8,128)(2,1)}, f32[1,4096]{1,0:T(1,128)}, f32[256,640]{1,0:T(8,128)}, f32[256,640]{1,0:T(8,128)}, f32[64,640]{1,0:T(8,128)}) custom-call(bf16[512,640]{1,0:T(8,128)(2,1)} %get-tuple-element.75.refs_0_, bf16[512,640]{1,0:T(8,128)(2,1)} %get-tuple-element.76.refs_1_, bf16[2048,640]{1,0:T(8,128)(2,1)} %get-tuple-element.60.refs_2_, ...), custom_call_target="tpu_custom_call" | custom-call | tf_op jit(solution)/shard_map/rec_back/pallas_call | solution.py:205
  444.9 8.3 %settle.1 = (bf16[512,2048]{1,0:T(8,128)(2,1)}, bf16[512,2048]{1,0:T(8,128)(2,1)}, f32[256,640]{1,0:T(8,128)}, f32[256,640]{1,0:T(8,128)}, f32[256,640]{1,0:T(8,...) custom-call(bf16[512,2048]{1,0:T(8,128)(2,1)} %get-tuple-element.74.refs_0_, ...), custom_call_target="tpu_custom_call" | custom-call | tf_op jit(solution)/shard_map/settle/pallas_call | solution.py:1355
  453.2 0.7 reshape.363
  453.9 0.7 reshape.364
  (78 shorter events, 12.3 us)
Async XLA Ops:
  41.5 4.0 copy-start.7
  48.1 5.2 %copy-start = (bf16[1,512,2048]{2,1,0:T(8,128)(2,1)S(1)}, bf16[1,512,2048]{2,1,0:T(8,128)(2,1)}, u32[]{:S(2)}) copy-start(bf16[1,512,2048]{2,1,0:T(8,128)(2,1)} %param.18) | copy-start | bytes 6291460
  53.9 2.3 copy-start.4
  54.4 4.6 copy-start.2
  56.1 2.9 copy-start.5
  170.8 9.3 %copy-start.1 = (bf16[1,512,2048]{2,1,0:T(8,128)(2,1)S(1)}, bf16[1,512,2048]{2,1,0:T(8,128)(2,1)}, u32[]{:S(2)}) copy-start(bf16[1,512,2048]{2,1,0:T(8,128)(2,1)} %param.20) | copy-start | bytes 6291460
  180.2 6.0 %copy-start.3 = (bf16[2048,1536]{1,0:T(8,128)(2,1)S(1)}, bf16[2048,1536]{1,0:T(8,128)(2,1)}, u32[]{:S(2)}) copy-start(bf16[2048,1536]{1,0:T(8,128)(2,1)} %get-tuple-element.63.refs_4_) | copy-start | bytes 18874372
  180.2 6.0 %copy-start.6 = (bf16[512,2048]{1,0:T(8,128)(2,1)S(1)}, bf16[512,2048]{1,0:T(8,128)(2,1)}, u32[]{:S(2)}) copy-start(bf16[512,2048]{1,0:T(8,128)(2,1)} %get-tuple-element.61.refs_0_) | copy-start | bytes 6291460
  180.2 6.1 %copy-start.10 = (f32[512,1536]{1,0:T(8,128)S(1)}, f32[512,1536]{1,0:T(8,128)}, u32[]{:S(2)}) copy-start(f32[512,1536]{1,0:T(8,128)} %fusion.23) | copy-start | bytes 9437188
  444.8 8.3 %copy-start.8 = (f32[64,640]{1,0:T(8,128)S(1)}, f32[64,640]{1,0:T(8,128)}, u32[]{:S(2)}) copy-start(f32[64,640]{1,0:T(8,128)} %get-tuple-element.94) | copy-start | bytes 491524
  444.9 10.4 %copy-start.9 = (f32[1,4096]{1,0:T(1,128)S(1)}, f32[1,4096]{1,0:T(1,128)}, u32[]{:S(2)}) copy-start(f32[1,4096]{1,0:T(1,128)} %get-tuple-element.91) | copy-start | bytes 49156
